TPU v7x, 32 devices: a whole 2x2x4 slice. The times are simulated.
32 devices in a mesh: dp: 8 (over y, x, core), tensor: 4 (over z).
Axes of the slice: x: 2, y: 2, z: 4, core: 2. Of those that a mesh axis runs over, the one named last changes fastest.
Arguments:
- inputs: bfloat16 [16384, 1024], P('dp'), may hold values from -6 to 6
- cotangent: bfloat16 [16384, 1024], P(('dp', 'tensor')), may hold values from -6 to 6
- lengths: int32 [16], P('dp'), may hold values from 256 to 1024, as said below
- query_weight: bfloat16 [1024, 1024], P(None, 'tensor'), may hold values from -0.1875 to 0.1875
- key_weight: bfloat16 [1024, 1024], P(None, 'tensor'), may hold values from -0.1875 to 0.1875
- value_weight: bfloat16 [1024, 1024], P(None, 'tensor'), may hold values from -0.1875 to 0.1875
- query_bias: float32 [1024], P('tensor'), may hold values from -3 to 3
- value_bias: float32 [1024], P('tensor'), may hold values from -3 to 3
- out_weight: bfloat16 [1024, 1024], P('tensor'), may hold values from -1 to 1
- out_bias: float32 [1024], replicated, may hold values from -3 to 3
- norm1_gain: float32 [1024], replicated, may hold values from 0.5 to 1.5
- norm1_bias: float32 [1024], replicated, may hold values from -2 to 2
- up_weight: bfloat16 [1024, 4096], P(None, 'tensor'), may hold values from -0.1875 to 0.1875
- up_bias: float32 [4096], P('tensor'), may hold values from -3 to 3
- down_weight: bfloat16 [4096, 1024], P('tensor'), may hold values from -0.09375 to 0.09375
- down_bias: float32 [1024], replicated, may hold values from -3 to 3
- norm2_gain: float32 [1024], replicated, may hold values from 0.5 to 1.5
- norm2_bias: float32 [1024], replicated, may hold values from -2 to 2
Outputs:
- outputs: bfloat16 [16384, 1024], P(('dp', 'tensor'))
- input_grad: float32 [16384, 1024], P(('dp', 'tensor'))
- query_weight_grad: float32 [1024, 1024], P(None, 'tensor')
- key_weight_grad: float32 [1024, 1024], P(None, 'tensor')
- value_weight_grad: float32 [1024, 1024], P(None, 'tensor')
- query_bias_grad: float32 [1024], P('tensor')
- value_bias_grad: float32 [1024], P('tensor')
- out_weight_grad: float32 [1024, 1024], P('tensor')
- out_bias_grad: float32 [1024], replicated
- norm1_gain_grad: float32 [1024], replicated
- norm1_bias_grad: float32 [1024], replicated
- up_weight_grad: float32 [1024, 4096], P(None, 'tensor')
- up_bias_grad: float32 [4096], P('tensor')
- down_weight_grad: float32 [4096, 1024], P('tensor')
- down_bias_grad: float32 [1024], replicated
- norm2_gain_grad: float32 [1024], replicated
- norm2_bias_grad: float32 [1024], replicated
Inputs may be any that keep to these rules, and one draw needn't show every extreme that they name: `lengths`: among the 2 sequences of each index of dp one has length 1024.
All inputs are finite; a program needn't handle non-finite values.
Results may differ from a plain program's by a relative error of at most 0.023.
Values may be sent and summed in bfloat16 or wider, within the bound.
A program may use at most 128 MiB of HBM per device.

v0:
```python
import jax
import jax.numpy as jnp
from jax import lax
from jax.sharding import PartitionSpec as P

HD = 64
LEN = 1024


def norm_forward(values, gain, bias):
    center = values - jnp.mean(values, axis=-1, keepdims=True)
    inverse = lax.rsqrt(jnp.mean(center * center, axis=-1, keepdims=True) + 1e-05)
    normal = center * inverse
    return (normal * gain + bias, normal, inverse)


def norm_backward(grad, normal, inverse, gain):
    scaled = grad * gain
    first_mean = jnp.mean(scaled, axis=-1, keepdims=True)
    second_mean = jnp.mean(scaled * normal, axis=-1, keepdims=True)
    return (
        inverse * (scaled - first_mean - normal * second_mean),
        jnp.sum(grad * normal, 0),
        jnp.sum(grad, 0),
    )


def length_of(lengths, sequence):
    return jnp.sum(jnp.where(jnp.arange(lengths.shape[0]) == sequence, lengths, 0))


def block_scores(query_block, key_seq, length):
    raw = jnp.einsum("qhd,khd->hqk", query_block, key_seq, preferred_element_type=jnp.float32)
    key_valid = jnp.arange(key_seq.shape[0]) < length
    return jnp.where(key_valid[None, None, :], raw * HD ** (-0.5), -1e30)


def block_slices(queries, keys, values, index, block_rows):
    width = queries.shape[1]
    heads_here = width // HD
    first_row = index * block_rows
    seq_first = first_row // LEN * LEN
    query_block = lax.dynamic_slice_in_dim(queries, first_row, block_rows, 0).reshape(
        block_rows, heads_here, HD
    )
    key_seq = lax.dynamic_slice_in_dim(keys, seq_first, LEN, 0).reshape(LEN, heads_here, HD)
    value_seq = lax.dynamic_slice_in_dim(values, seq_first, LEN, 0).reshape(LEN, heads_here, HD)
    return (first_row, seq_first, query_block, key_seq, value_seq)


def attend_forward(queries, keys, values, lengths, block_rows):
    row_count, width = queries.shape

    def attend_block(index):
        first_row, seq_first, query_block, key_seq, value_seq = block_slices(
            queries, keys, values, index, block_rows
        )
        scores = block_scores(query_block, key_seq, length_of(lengths, first_row // LEN))
        row_max = jnp.max(scores, axis=-1, keepdims=True)
        exponent = jnp.exp(scores - row_max)
        row_total = jnp.sum(exponent, axis=-1, keepdims=True)
        probs = (exponent / row_total).astype(jnp.bfloat16)
        attended = jnp.einsum("hqk,khd->qhd", probs, value_seq, preferred_element_type=jnp.float32)
        return (attended.reshape(block_rows, width), row_max + jnp.log(row_total))

    attended, log_total = lax.map(attend_block, jnp.arange(row_count // block_rows))
    return (attended.reshape(row_count, width), log_total)


def attend_backward(queries, keys, values, d_attended, log_total, lengths, block_rows):
    row_count, width = queries.shape
    heads_here = width // HD

    def back_block(sums, index):
        key_grad, value_grad = sums
        first_row, seq_first, query_block, key_seq, value_seq = block_slices(
            queries, keys, values, index, block_rows
        )
        d_block = lax.dynamic_slice_in_dim(d_attended, first_row, block_rows, 0).reshape(
            block_rows, heads_here, HD
        )
        scores = block_scores(query_block, key_seq, length_of(lengths, first_row // LEN))
        probs = jnp.exp(scores - log_total[index])
        d_probs = jnp.einsum("qhd,khd->hqk", d_block, value_seq, preferred_element_type=jnp.float32)
        inner = jnp.sum(probs * d_probs, axis=-1, keepdims=True)
        d_scores = (probs * (d_probs - inner) * HD ** (-0.5)).astype(jnp.bfloat16)
        value_part = jnp.einsum(
            "hqk,qhd->khd", probs.astype(jnp.bfloat16), d_block, preferred_element_type=jnp.float32
        ).reshape(LEN, width)
        key_part = jnp.einsum(
            "hqk,qhd->khd", d_scores, query_block, preferred_element_type=jnp.float32
        ).reshape(LEN, width)
        query_part = jnp.einsum(
            "hqk,khd->qhd", d_scores, key_seq, preferred_element_type=jnp.float32
        ).reshape(block_rows, width)
        key_grad = lax.dynamic_update_slice_in_dim(
            key_grad, lax.dynamic_slice_in_dim(key_grad, seq_first, LEN, 0) + key_part, seq_first, 0
        )
        value_grad = lax.dynamic_update_slice_in_dim(
            value_grad,
            lax.dynamic_slice_in_dim(value_grad, seq_first, LEN, 0) + value_part,
            seq_first,
            0,
        )
        return ((key_grad, value_grad), query_part)

    zeros = jnp.zeros((row_count, width), jnp.float32)
    (key_grad, value_grad), query_grad = lax.scan(
        back_block, (zeros, zeros), jnp.arange(row_count // block_rows)
    )
    return (
        query_grad.reshape(row_count, width).astype(jnp.bfloat16),
        key_grad.astype(jnp.bfloat16),
        value_grad.astype(jnp.bfloat16),
    )


def exact_gelu(values):
    return jax.nn.gelu(values, approximate=False)


def on_device(
    inputs,
    cotangent,
    lengths,
    query_weight,
    key_weight,
    value_weight,
    query_bias,
    value_bias,
    out_weight,
    out_bias,
    norm1_gain,
    norm1_bias,
    up_weight,
    up_bias,
    down_weight,
    down_bias,
    norm2_gain,
    norm2_bias,
):
    tensor_size = lax.axis_size("tensor")
    tensor_pos = lax.axis_index("tensor")
    row_count = inputs.shape[0]
    share_rows = row_count // tensor_size
    first_share = tensor_pos * share_rows
    block_rows = min(512, LEN)
    queries = (
        jnp.dot(inputs, query_weight, preferred_element_type=jnp.float32) + query_bias
    ).astype(jnp.bfloat16)
    keys = jnp.dot(inputs, key_weight, preferred_element_type=jnp.float32).astype(jnp.bfloat16)
    values = (
        jnp.dot(inputs, value_weight, preferred_element_type=jnp.float32) + value_bias
    ).astype(jnp.bfloat16)
    attended, log_total = attend_forward(queries, keys, values, lengths, block_rows)
    attended_low = attended.astype(jnp.bfloat16)
    piece = attended_low
    attn_share = lax.psum_scatter(
        jnp.dot(piece, out_weight, preferred_element_type=jnp.float32).astype(jnp.bfloat16),
        "tensor",
        scatter_dimension=0,
        tiled=True,
    ).astype(jnp.float32)
    input_share = lax.dynamic_slice_in_dim(inputs, first_share, share_rows, 0).astype(jnp.float32)
    first = input_share + attn_share + out_bias
    normed1, normal1, inverse1 = norm_forward(first, norm1_gain, norm1_bias)
    hidden_low = lax.all_gather(normed1.astype(jnp.bfloat16), "tensor", axis=0, tiled=True)
    upper = jnp.dot(hidden_low, up_weight, preferred_element_type=jnp.float32) + up_bias
    active_low = exact_gelu(upper).astype(jnp.bfloat16)
    piece = active_low
    mlp_share = lax.psum_scatter(
        jnp.dot(piece, down_weight, preferred_element_type=jnp.float32).astype(jnp.bfloat16),
        "tensor",
        scatter_dimension=0,
        tiled=True,
    ).astype(jnp.float32)
    second = normed1 + mlp_share + down_bias
    outputs, normal2, inverse2 = norm_forward(second, norm2_gain, norm2_bias)
    row_index = first_share + jnp.arange(share_rows)
    row_seq = row_index // LEN
    row_length = jnp.sum(
        jnp.where(row_seq[:, None] == jnp.arange(lengths.shape[0])[None, :], lengths[None, :], 0), 1
    )
    row_valid = (row_index % LEN < row_length).astype(jnp.float32)
    grad_out = cotangent.astype(jnp.float32) * row_valid[:, None]
    d_second, norm2_gain_part, norm2_bias_part = norm_backward(
        grad_out, normal2, inverse2, norm2_gain
    )
    down_bias_part = jnp.sum(d_second, 0)
    d_second_low = lax.all_gather(d_second.astype(jnp.bfloat16), "tensor", axis=0, tiled=True)
    down_weight_grad = jnp.dot(active_low.T, d_second_low, preferred_element_type=jnp.float32)
    d_active = jnp.dot(d_second_low, down_weight.T, preferred_element_type=jnp.float32)
    gelu_pull = jax.vjp(exact_gelu, upper)[1]
    d_upper = gelu_pull(d_active)[0].astype(jnp.bfloat16)
    up_weight_grad = jnp.dot(hidden_low.T, d_upper, preferred_element_type=jnp.float32)
    up_bias_grad = jnp.sum(d_upper.astype(jnp.float32), 0)
    piece = d_upper
    d_normed1 = (
        lax.psum_scatter(
            jnp.dot(piece, up_weight.T, preferred_element_type=jnp.float32).astype(jnp.bfloat16),
            "tensor",
            scatter_dimension=0,
            tiled=True,
        ).astype(jnp.float32)
        + d_second
    )
    d_first, norm1_gain_part, norm1_bias_part = norm_backward(
        d_normed1, normal1, inverse1, norm1_gain
    )
    out_bias_part = jnp.sum(d_first, 0)
    d_first_low = lax.all_gather(d_first.astype(jnp.bfloat16), "tensor", axis=0, tiled=True)
    out_weight_grad = jnp.dot(attended_low.T, d_first_low, preferred_element_type=jnp.float32)
    d_attended = jnp.dot(d_first_low, out_weight.T, preferred_element_type=jnp.float32).astype(
        jnp.bfloat16
    )
    d_queries, d_keys, d_values = attend_backward(
        queries, keys, values, d_attended, log_total, lengths, block_rows
    )
    query_weight_grad = jnp.dot(inputs.T, d_queries, preferred_element_type=jnp.float32)
    key_weight_grad = jnp.dot(inputs.T, d_keys, preferred_element_type=jnp.float32)
    value_weight_grad = jnp.dot(inputs.T, d_values, preferred_element_type=jnp.float32)
    query_bias_grad = jnp.sum(d_queries.astype(jnp.float32), 0)
    value_bias_grad = jnp.sum(d_values.astype(jnp.float32), 0)
    total = jnp.dot(d_queries, query_weight.T, preferred_element_type=jnp.float32)
    total = total + jnp.dot(d_keys, key_weight.T, preferred_element_type=jnp.float32)
    input_grad = (
        lax.psum_scatter(
            (total + jnp.dot(d_values, value_weight.T, preferred_element_type=jnp.float32)).astype(
                jnp.bfloat16
            ),
            "tensor",
            scatter_dimension=0,
            tiled=True,
        ).astype(jnp.float32)
        + d_first
    )
    (
        query_weight_grad,
        key_weight_grad,
        value_weight_grad,
        query_bias_grad,
        value_bias_grad,
        out_weight_grad,
        up_weight_grad,
        up_bias_grad,
        down_weight_grad,
    ) = lax.psum(
        (
            query_weight_grad,
            key_weight_grad,
            value_weight_grad,
            query_bias_grad,
            value_bias_grad,
            out_weight_grad,
            up_weight_grad,
            up_bias_grad,
            down_weight_grad,
        ),
        "dp",
    )
    (
        norm1_gain_grad,
        norm1_bias_grad,
        norm2_gain_grad,
        norm2_bias_grad,
        out_bias_grad,
        down_bias_grad,
    ) = lax.psum(
        (
            norm1_gain_part,
            norm1_bias_part,
            norm2_gain_part,
            norm2_bias_part,
            out_bias_part,
            down_bias_part,
        ),
        ("dp", "tensor"),
    )
    return (
        outputs.astype(jnp.bfloat16),
        input_grad,
        query_weight_grad,
        key_weight_grad,
        value_weight_grad,
        query_bias_grad,
        value_bias_grad,
        out_weight_grad,
        out_bias_grad,
        norm1_gain_grad,
        norm1_bias_grad,
        up_weight_grad,
        up_bias_grad,
        down_weight_grad,
        down_bias_grad,
        norm2_gain_grad,
        norm2_bias_grad,
    )


def solution(mesh):
    return jax.shard_map(
        on_device,
        mesh=mesh,
        in_specs=(
            P("dp", None),
            P(("dp", "tensor"), None),
            P("dp"),
            P(None, "tensor"),
            P(None, "tensor"),
            P(None, "tensor"),
            P("tensor"),
            P("tensor"),
            P("tensor", None),
            P(),
            P(),
            P(),
            P(None, "tensor"),
            P("tensor"),
            P("tensor", None),
            P(),
            P(),
            P(),
        ),
        out_specs=(
            P(("dp", "tensor"), None),
            P(("dp", "tensor"), None),
            P(None, "tensor"),
            P(None, "tensor"),
            P(None, "tensor"),
            P("tensor"),
            P("tensor"),
            P("tensor", None),
            P(),
            P(),
            P(),
            P(None, "tensor"),
            P("tensor"),
            P("tensor", None),
            P(),
            P(),
            P(),
        ),
        check_vma=False,
    )
```

profile of v0, /device:TPU:0, one launch (start us, length us, event | category | flops | bytes accessed | tf_op | source)
XLA Modules:
  0.0 1227.8 jit_solution(2095789739427031285)
XLA Ops:
  26.3 52.2 %while.30 = (s32[]{:T(128)}, bf16[4,512,256]{2,1,0:T(8,128)(2,1)}, f32[4,4,512,1]{2,1,3,0:T(4,128)S(1)}, s32[4]{0:T(128)S(1)}, bf16[2048,256]{0,1:T(8,128)(2,1)S...) while((s32[]{:T(128)}, bf16[4,512,256]{2,1,0:T(8,128)(2,1)}, ...), condition=%wide.region_4.5_spmd, body=%wide.region_0.4_spmd.sunk | while | flops 562035712 | bytes 30478772 | solution.py:66
  83.3 79.5 %reduce-scatter.5.cloned.1.call-done = bf16[512,1024]{1,0:T(8,128)(2,1)} async-done(((bf16[2048,1024]{1,0:T(8,128)(2,1)}), bf16[512,1024]{1,0:T(8,128)(2,1)}) %reduce-scatter.5.cloned.1.call-update) | async-done | bytes 1048592 | tf_op jit(solution)/shard_map/reduce_scatter | solution.py:158
  170.1 81.2 %all-gather.4.cloned.1.call-done = bf16[2048,1024]{1,0:T(8,128)(2,1)} async-done(((bf16[512,1024]{1,0:T(8,128)(2,1)}), bf16[2048,1024]{1,0:T(8,128)(2,1)}) %all-gather.4.cloned.1.call-update) | async-done | bytes 4194320 | tf_op jit(solution)/shard_map/all_gather | solution.py:167
  251.3 25.4 %multiply_convert_fusion.1 = (bf16[2048,1024]{1,0:T(8,128)(2,1)S(1)}, f32[2048,1024]{1,0:T(8,128)}, f32[2048,1024]{1,0:T(8,128)}) fusion(f32[1024]{0:T(1024)S(1)} %copy-done.40, bf16[2048,1024]{1,0:T(8,128)(2,1)} %all-gather.4.cloned.1.call-done, bf16[1024,1024]{1,0:T(8,128)(2,1)S(1)} %copy-done), kind=kOutput, calls=%fused_computation.60 | convolution fusion | flops 4433379328 | bytes 27267072 | tf_op jit(solution)/shard_map/dot_general | solution.py:168
  284.8 75.3 %reduce-scatter.7.cloned.1.call-done = bf16[512,1024]{1,0:T(8,128)(2,1)} async-done(((bf16[2048,1024]{1,0:T(8,128)(2,1)}), bf16[512,1024]{1,0:T(8,128)(2,1)}) %reduce-scatter.7.cloned.1.call-update) | async-done | bytes 1048592 | tf_op jit(solution)/shard_map/reduce_scatter | solution.py:171
  368.1 81.0 %all-gather.6.cloned.1.call-done = bf16[2048,1024]{1,0:T(8,128)(2,1)} async-done(((bf16[512,1024]{1,0:T(8,128)(2,1)}), bf16[2048,1024]{1,0:T(8,128)(2,1)}) %all-gather.6.cloned.1.call-update) | async-done | bytes 4194320 | tf_op jit(solution)/shard_map/all_gather | solution.py:190
  449.1 13.9 %convert_reduce_fusion = (f32[1024]{0:T(1024)}, bf16[2048,1024]{1,0:T(8,128)(2,1)S(1)}) fusion(f32[2048,1024]{1,0:T(8,128)} %get-tuple-element.444, f32[2048,1024]{1,0:T(8,128)} %get-tuple-element.452, f32[1024]{0:T(1024)S(1)} %copy-done.40, bf16[2048,1024]{1,0:T(8,128)(2,1)} %all-gather.6.cloned.1.call-done, bf16[1024,1024]{1,0:T(8,128)(2,1)} %param.36), kind=kOutput, calls=%fused_computation.57 | convolution fusion | flops 4330617856 | bytes 27271168 | tf_op jit(solution)/shard_map/dot_general | solution.py:192
  471.3 75.4 %reduce-scatter.9.cloned.1.call-done = bf16[512,1024]{1,0:T(8,128)(2,1)} async-done(((bf16[2048,1024]{1,0:T(8,128)(2,1)}), bf16[512,1024]{1,0:T(8,128)(2,1)}) %reduce-scatter.9.cloned.1.call-update) | async-done | bytes 1048592 | tf_op jit(solution)/shard_map/reduce_scatter | solution.py:199
  556.6 10.1 fusion.83
  572.8 65.0 %all-gather.8.cloned.1.call-done = bf16[2048,1024]{1,0:T(8,128)(2,1)} async-done(((bf16[512,1024]{1,0:T(8,128)(2,1)}), bf16[2048,1024]{1,0:T(8,128)(2,1)}) %all-gather.8.cloned.1.call-update) | async-done | bytes 4194320 | tf_op jit(solution)/shard_map/all_gather | solution.py:211
  645.2 298.9 %while.31 = (s32[]{:T(128)}, f32[2048,256]{0,1:T(8,128)}, f32[2048,256]{0,1:T(8,128)S(1)}, bf16[4,512,256]{2,1,0:T(8,128)(2,1)}, s32[4]{0:T(128)S(1)}, /*index=5...) while((s32[]{:T(128)}, f32[2048,256]{0,1:T(8,128)}, ...), condition=%wide.region_20.21_spmd, body=%wide.region_17.20_spmd.sunk | while | flops 1397234688 | bytes 84193872 | solution.py:108
  663.9 22.0 %fusion.171 = bf16[4,64,512]{2,1,0:T(8,128)(2,1)} fusion(bf16[1024,4,64]{0,2,1:T(8,128)(2,1)S(1)} %bitcast.125, f32[4,512,1024]{2,1,0:T(8,128)} %fusion.169, f32[4,512,1024]{2,1,0:T(8,128)} %fusion.166, f32[4,512]{1,0:T(4,128)S(1)} %dynamic-slice_bitcast_fusion.2, pred[1024]{0:T(1024)(128)(4,1)S(1)} %iota_compare_fusion.5), kind=kOutput, calls=%fused_computation.22.clone.1 | convolution fusion | flops 291507200 | bytes 17572864 | tf_op jit(solution)/shard_map/while/body/eval_jaxpr/hqk,khd->qhd/dot_general | solution.py:93
  685.9 22.7 %fusion.170 = f32[4,64,1024]{2,1,0:T(8,128)} fusion(bf16[512,4,64]{0,2,1:T(8,128)(2,1)S(1)} %bitcast.129, f32[4,512,1024]{2,1,0:T(8,128)} %fusion.169, f32[4,512,1024]{2,1,0:T(8,128)} %fusion.166, f32[4,512]{1,0:T(4,128)S(1)} %dynamic-slice_bitcast_fusion.2, pred[1024]{0:T(1024)(128)(4,1)S(1)} %iota_compare_fusion.5), kind=kOutput, calls=%fused_computation.23.clone.1 | convolution fusion | flops 291507200 | bytes 18097152 | tf_op jit(solution)/shard_map/while/body/eval_jaxpr/hqk,qhd->khd/dot_general | solution.py:90
  738.5 22.0 %fusion.171 = bf16[4,64,512]{2,1,0:T(8,128)(2,1)} fusion(bf16[1024,4,64]{0,2,1:T(8,128)(2,1)S(1)} %bitcast.125, f32[4,512,1024]{2,1,0:T(8,128)} %fusion.169, f32[4,512,1024]{2,1,0:T(8,128)} %fusion.166, f32[4,512]{1,0:T(4,128)S(1)} %dynamic-slice_bitcast_fusion.2, pred[1024]{0:T(1024)(128)(4,1)S(1)} %iota_compare_fusion.5), kind=kOutput, calls=%fused_computation.22.clone.1 | convolution fusion | flops 291507200 | bytes 17572864 | tf_op jit(solution)/shard_map/while/body/eval_jaxpr/hqk,khd->qhd/dot_general | solution.py:93
  760.5 22.7 %fusion.170 = f32[4,64,1024]{2,1,0:T(8,128)} fusion(bf16[512,4,64]{0,2,1:T(8,128)(2,1)S(1)} %bitcast.129, f32[4,512,1024]{2,1,0:T(8,128)} %fusion.169, f32[4,512,1024]{2,1,0:T(8,128)} %fusion.166, f32[4,512]{1,0:T(4,128)S(1)} %dynamic-slice_bitcast_fusion.2, pred[1024]{0:T(1024)(128)(4,1)S(1)} %iota_compare_fusion.5), kind=kOutput, calls=%fused_computation.23.clone.1 | convolution fusion | flops 291507200 | bytes 18097152 | tf_op jit(solution)/shard_map/while/body/eval_jaxpr/hqk,qhd->khd/dot_general | solution.py:90
  783.2 6.3 fusion.168
  813.1 22.0 %fusion.171 = bf16[4,64,512]{2,1,0:T(8,128)(2,1)} fusion(bf16[1024,4,64]{0,2,1:T(8,128)(2,1)S(1)} %bitcast.125, f32[4,512,1024]{2,1,0:T(8,128)} %fusion.169, f32[4,512,1024]{2,1,0:T(8,128)} %fusion.166, f32[4,512]{1,0:T(4,128)S(1)} %dynamic-slice_bitcast_fusion.2, pred[1024]{0:T(1024)(128)(4,1)S(1)} %iota_compare_fusion.5), kind=kOutput, calls=%fused_computation.22.clone.1 | convolution fusion | flops 291507200 | bytes 17572864 | tf_op jit(solution)/shard_map/while/body/eval_jaxpr/hqk,khd->qhd/dot_general | solution.py:93
  835.1 22.7 %fusion.170 = f32[4,64,1024]{2,1,0:T(8,128)} fusion(bf16[512,4,64]{0,2,1:T(8,128)(2,1)S(1)} %bitcast.129, f32[4,512,1024]{2,1,0:T(8,128)} %fusion.169, f32[4,512,1024]{2,1,0:T(8,128)} %fusion.166, f32[4,512]{1,0:T(4,128)S(1)} %dynamic-slice_bitcast_fusion.2, pred[1024]{0:T(1024)(128)(4,1)S(1)} %iota_compare_fusion.5), kind=kOutput, calls=%fused_computation.23.clone.1 | convolution fusion | flops 291507200 | bytes 18097152 | tf_op jit(solution)/shard_map/while/body/eval_jaxpr/hqk,qhd->khd/dot_general | solution.py:90
  887.7 22.0 %fusion.171 = bf16[4,64,512]{2,1,0:T(8,128)(2,1)} fusion(bf16[1024,4,64]{0,2,1:T(8,128)(2,1)S(1)} %bitcast.125, f32[4,512,1024]{2,1,0:T(8,128)} %fusion.169, f32[4,512,1024]{2,1,0:T(8,128)} %fusion.166, f32[4,512]{1,0:T(4,128)S(1)} %dynamic-slice_bitcast_fusion.2, pred[1024]{0:T(1024)(128)(4,1)S(1)} %iota_compare_fusion.5), kind=kOutput, calls=%fused_computation.22.clone.1 | convolution fusion | flops 291507200 | bytes 17572864 | tf_op jit(solution)/shard_map/while/body/eval_jaxpr/hqk,khd->qhd/dot_general | solution.py:93
  909.7 22.7 %fusion.170 = f32[4,64,1024]{2,1,0:T(8,128)} fusion(bf16[512,4,64]{0,2,1:T(8,128)(2,1)S(1)} %bitcast.129, f32[4,512,1024]{2,1,0:T(8,128)} %fusion.169, f32[4,512,1024]{2,1,0:T(8,128)} %fusion.166, f32[4,512]{1,0:T(4,128)S(1)} %dynamic-slice_bitcast_fusion.2, pred[1024]{0:T(1024)(128)(4,1)S(1)} %iota_compare_fusion.5), kind=kOutput, calls=%fused_computation.23.clone.1 | convolution fusion | flops 291507200 | bytes 18097152 | tf_op jit(solution)/shard_map/while/body/eval_jaxpr/hqk,qhd->khd/dot_general | solution.py:90
  965.6 41.0 %all-reduce = (f32[1024]{0:T(1024)}, f32[1024]{0:T(1024)}, f32[1024]{0:T(1024)}, f32[1024]{0:T(1024)}, f32[1024]{0:T(1024)}, /*index=5*/f32[1024]{0:T(1024)}) all-reduce(f32[1024]{0:T(1024)S(1)} %copy-done.25, f32[1024]{0:T(1024)S(1)} %copy-done.29, f32[1024]{0:T(1024)S(1)} %copy-done.30, ...), channel_id=1, replica_groups=mesh['dp'=8,'tensor'=4] {'dp','tensor'}, use_global_device_ids=true, to_apply=%region_31.32 | all-reduce | flops 6144 | bytes 49152 | tf_op jit(solution)/shard_map/psum | solution.py:268
  1007.1 14.6 %all-reduce.1 = (f32[256]{0:T(256)}, f32[256]{0:T(256)}, f32[1024]{0:T(1024)}) all-reduce(f32[256]{0:T(256)S(1)} %convert_reduce_fusion.2, f32[256]{0:T(256)S(1)} %convert_reduce_fusion.1, f32[1024]{0:T(1024)S(1)} %copy-done.34), channel_id=1, replica_groups=mesh['dp'=8,'tensor'=4] {'dp'}, use_global_device_ids=true, to_apply=%region_26.27 | all-reduce | flops 1536 | bytes 12288 | tf_op jit(solution)/shard_map/psum | solution.py:247
  1021.7 109.2 %all-reduce.5.cloned.1.call-done = (f32[1024,256]{0,1:T(8,128)}, f32[1024,256]{0,1:T(8,128)}, f32[1024,256]{0,1:T(8,128)}, f32[256,1024]{1,0:T(8,128)}, f32[1024,1024]{1,0:T(8,128)}, /*index=5*/f32[1024,1024]{1,0:T(8,128)}) async-done(((f32[1024,256]{0,1:T(8,128)}, f32[1024,256]{0,1:T(8,128)}, f32[1024,256]{0,1:T(8,128)}, f32[256,1024]{1,0:T(8,128)}, f32[1024,1024]{1,0:T(8,128)}, ...) | async-done | bytes 12582928 | tf_op jit(solution)/shard_map/psum | solution.py:247
  1138.5 72.1 %reduce-scatter.11.cloned.1.call-done = bf16[512,1024]{1,0:T(8,128)(2,1)} async-done(((bf16[2048,1024]{1,0:T(8,128)(2,1)}), bf16[512,1024]{1,0:T(8,128)(2,1)}) %reduce-scatter.11.cloned.1.call-update) | async-done | bytes 1048592 | tf_op jit(solution)/shard_map/reduce_scatter | solution.py:227
  (281 shorter events, 270.2 us)
Async XLA Ops:
  7.2 244.1 %copy-start = (bf16[1024,1024]{1,0:T(8,128)(2,1)S(1)}, bf16[1024,1024]{1,0:T(8,128)(2,1)}, u32[]{:S(2)}) copy-start(bf16[1024,1024]{1,0:T(8,128)(2,1)} %param.34) | copy-start | bytes 6291460
  7.2 155.6 %reduce-scatter.5.cloned.1.call-start = ((), (), s32[]{:S(2)}) async-start(), calls=%async_computation.4 | async-start | bytes 5242880 | tf_op jit(solution)/shard_map/reduce_scatter | solution.py:158
  83.2 79.6 %copy-start.23 = (f32[1024]{0:T(1024)S(1)}, f32[1024]{0:T(1024)}, u32[]{:S(2)}) copy-start(f32[1024]{0:T(1024)} %param.31) | copy-start | bytes 12292
  83.2 83.8 %copy-start.24 = (f32[1024]{0:T(1024)S(1)}, f32[1024]{0:T(1024)}, u32[]{:S(2)}) copy-start(f32[1024]{0:T(1024)} %param.32) | copy-start | bytes 12292
  83.2 83.8 %copy-start.32 = (f32[1024]{0:T(1024)S(1)}, f32[1024]{0:T(1024)}, u32[]{:S(2)}) copy-start(f32[1024]{0:T(1024)} %param.33) | copy-start | bytes 12292
  83.2 168.1 %all-gather.4.cloned.1.call-start = ((), (), s32[]{:S(2)}) async-start(), calls=%async_computation.5 | async-start | bytes 5242880 | tf_op jit(solution)/shard_map/all_gather | solution.py:167
  83.2 168.0 %copy-start.40 = (f32[1024]{0:T(1024)S(1)}, f32[1024]{0:T(1024)}, u32[]{:S(2)}) copy-start(f32[1024]{0:T(1024)} %param.35) | copy-start | bytes 12292
  169.8 190.3 %reduce-scatter.7.cloned.1.call-start = ((), (), s32[]{:S(2)}) async-start(), calls=%async_computation.6 | async-start | bytes 5242880 | tf_op jit(solution)/shard_map/reduce_scatter | solution.py:171
  251.3 27.4 %copy-start.39 = (bf16[1024,1024]{1,0:T(8,128)(2,1)S(1)}, bf16[1024,1024]{1,0:T(8,128)(2,1)}, u32[]{:S(2)}) copy-start(bf16[1024,1024]{1,0:T(8,128)(2,1)} %param.36) | copy-start | bytes 6291460
  284.6 75.5 %copy-start.35 = (f32[1024]{0:T(1024)S(1)}, f32[1024]{0:T(1024)}, u32[]{:S(2)}) copy-start(f32[1024]{0:T(1024)} %param.37) | copy-start | bytes 12292
  284.7 78.8 %copy-start.26 = (f32[1024]{0:T(1024)S(1)}, f32[1024]{0:T(1024)}, u32[]{:S(2)}) copy-start(f32[1024]{0:T(1024)} %param.38) | copy-start | bytes 12292
  284.7 164.4 %all-gather.6.cloned.1.call-start = ((), (), s32[]{:S(2)}) async-start(), calls=%async_computation.7 | async-start | bytes 5242880 | tf_op jit(solution)/shard_map/all_gather | solution.py:190
  284.8 80.3 %copy-start.33 = (f32[1024]{0:T(1024)S(1)}, f32[1024]{0:T(1024)}, u32[]{:S(2)}) copy-start(f32[1024]{0:T(1024)} %param.39) | copy-start | bytes 12292
  367.7 179.0 %reduce-scatter.9.cloned.1.call-start = ((), (), s32[]{:S(2)}) async-start(), calls=%async_computation.8 | async-start | bytes 5242880 | tf_op jit(solution)/shard_map/reduce_scatter | solution.py:199
  471.2 75.5 %copy-start.7 = (bf16[512,1024]{1,0:T(8,128)(2,1)S(1)}, bf16[512,1024]{1,0:T(8,128)(2,1)}, u32[]{:S(2)}) copy-start(bf16[512,1024]{1,0:T(8,128)(2,1)} %reduce-scatter.5.cloned.1.call-done) | copy-start | bytes 3145732
  471.2 166.5 %all-gather.8.cloned.1.call-start = ((), (), s32[]{:S(2)}) async-start(), calls=%async_computation.9 | async-start | bytes 5242880 | tf_op jit(solution)/shard_map/all_gather | solution.py:211
  556.4 574.5 %all-reduce.5.cloned.1.call-start = ((), (), s32[]{:S(2)}) async-start(), calls=%async_computation.11 | async-start | bytes 25165824 | tf_op jit(solution)/shard_map/psum | solution.py:247
  566.7 71.1 %copy-start.20 = (bf16[256,1024]{1,0:T(8,128)(2,1)S(1)}, bf16[256,1024]{1,0:T(8,128)(2,1)}, u32[]{:S(2)}) copy-start(bf16[256,1024]{1,0:T(8,128)(2,1)} %param.30) | copy-start | bytes 1572868
  760.5 22.7 %copy-start.8 = (bf16[512,256]{0,1:T(8,128)(2,1)S(1)}, bf16[512,256]{0,1:T(8,128)(2,1)}, u32[]{:S(2)}) copy-start(bf16[512,256]{0,1:T(8,128)(2,1)} %copy.95) | copy-start | bytes 786436 | tf_op jit(solution)/shard_map/while
  835.1 22.7 %copy-start.8 = (bf16[512,256]{0,1:T(8,128)(2,1)S(1)}, bf16[512,256]{0,1:T(8,128)(2,1)}, u32[]{:S(2)}) copy-start(bf16[512,256]{0,1:T(8,128)(2,1)} %copy.95) | copy-start | bytes 786436 | tf_op jit(solution)/shard_map/while
  956.4 254.3 %reduce-scatter.11.cloned.1.call-start = ((), (), s32[]{:S(2)}) async-start(), calls=%async_computation.10 | async-start | bytes 5242880 | tf_op jit(solution)/shard_map/reduce_scatter | solution.py:227
  964.9 42.2 %copy-start.34 = (f32[1024]{0:T(1024)S(1)}, f32[1024]{0:T(1024)}, u32[]{:S(2)}) copy-start(f32[1024]{0:T(1024)} %get-tuple-element.437) | copy-start | bytes 12292
  1007.1 203.6 %copy-start.10 = (f32[512,1024]{1,0:T(8,128)S(1)}, f32[512,1024]{1,0:T(8,128)}, u32[]{:S(2)}) copy-start(f32[512,1024]{1,0:T(8,128)} %copy-done.9) | copy-start | bytes 6291460
  1135.9 77.9 %copy-start.19 = (f32[256,1024]{1,0:T(8,128)S(1)}, f32[256,1024]{1,0:T(8,128)}, u32[]{:S(2)}) copy-start(f32[256,1024]{1,0:T(8,128)} %get-tuple-element.698) | copy-start | bytes 3145732
  (38 other events, 190.7 us)
Sparse Core Ops, SparseCore 0:
  83.3 79.4 reduce-scatter.4
  170.0 81.2 all-gather.3
  284.8 75.2 reduce-scatter.6
  367.8 81.2 all-gather.5
  471.4 75.2 reduce-scatter.8
  556.5 81.2 all-gather.7
  956.5 174.3 all-reduce.4
  1133.7 76.8 reduce-scatter.10
where the time goes:
time: 1240 us; the launch traced here: 1230 us
  waiting for transfers between devices  639 us (52%)
  matrix products  371 us (30%)
  local copies, waits for them, and re-layouts  75.2 us (6%)
  other arithmetic  57.7 us (5%)
  blocking collectives  55.6 us (4%)
  between operations  14.9 us (1%)
  loops' own time  14 us (1%)
    psum x1, waiting for transfers between devices, on_device(): lax.psum((query_weight_grad, key_weight_grad, value_weight_grad, query_bi...  109 us
    dot_general x4, matrix products, back_block(): jnp.einsum('hqk,qhd->khd', d_scores, query_block, preferred_element_type=...  90.8 us
    dot_general x4, matrix products, back_block(): jnp.einsum('hqk,khd->qhd', d_scores, key_seq, preferred_element_type=jnp....  88.1 us
    all_gather x1, waiting for transfers between devices, on_device(): lax.all_gather(normed1.astype(jnp.bfloat16), 'tensor', axis=0, tiled=True)  81.2 us
    all_gather x1, waiting for transfers between devices, on_device(): lax.all_gather(d_second.astype(jnp.bfloat16), 'tensor', axis=0, tiled=True)  81 us
    reduce_scatter x1, waiting for transfers between devices, on_device(): lax.psum_scatter(jnp.dot(piece, out_weight, preferred_element_type=jnp.fl...  79.5 us
    reduce_scatter x1, waiting for transfers between devices, on_device(): lax.psum_scatter(jnp.dot(piece, up_weight.T, preferred_element_type=jnp.f...  75.4 us
    reduce_scatter x1, waiting for transfers between devices, on_device(): lax.psum_scatter(jnp.dot(piece, down_weight, preferred_element_type=jnp.f...  75.3 us
  transfers between devices with their start and end apart: 8, of which 8 were waited for; matrix products, arithmetic and copies ran while one was open for 3% of the time, Pallas kernels for 0%

commit v1 on v0

v1 whole, which is shorter than its diff:
```python
import functools

import jax
import jax.numpy as jnp
from jax import lax
from jax.experimental import pallas as pl
from jax.experimental.pallas import tpu as pltpu
from jax.sharding import PartitionSpec as P

HD = 64
LEN = 1024
PAIR = 2 * HD
F32 = jnp.float32
BF = jnp.bfloat16
NN = (((1,), (0,)), ((), ()))
NT = (((1,), (1,)), ((), ()))
TN = (((0,), (0,)), ((), ()))


def product(left, right, dims=NN):
    return lax.dot_general(left, right, dims, preferred_element_type=F32)


def attend_forward_kernel(
    block,
    len_ref,
    x_ref,
    wq_ref,
    wk_ref,
    wv_ref,
    bq_ref,
    bv_ref,
    q_ref,
    k_ref,
    v_ref,
    o_ref,
    lse_ref,
):
    rows, width = q_ref.shape
    proj_rows = 256

    def project(index, carry):
        at = pl.ds(pl.multiple_of(index * proj_rows, proj_rows), proj_rows)
        x = x_ref[at, :]
        queries = (product(x, wq_ref[...]) + bq_ref[...]).astype(BF)
        q_ref[at, :] = (queries.astype(F32) * HD ** (-0.5)).astype(BF)
        k_ref[at, :] = product(x, wk_ref[...]).astype(BF)
        v_ref[at, :] = (product(x, wv_ref[...]) + bv_ref[...]).astype(BF)
        return carry

    lax.fori_loop(0, rows // proj_rows, project, 0)
    blocks_per_seq = LEN // block

    def attend(index, carry):
        seq = index // blocks_per_seq
        keys_at = pl.ds(pl.multiple_of(seq * LEN, LEN), LEN)
        rows_at = pl.ds(pl.multiple_of(index * block, block), block)
        length = len_ref[seq]
        key_slot = lax.broadcasted_iota(jnp.int32, (LEN, block), 0)
        lane = lax.broadcasted_iota(jnp.int32, (block, PAIR), 1)
        for pair in range(width // PAIR):
            cols = slice(pair * PAIR, (pair + 1) * PAIR)
            keys, values, queries = k_ref[keys_at, cols], v_ref[keys_at, cols], q_ref[rows_at, cols]
            parts = []
            for head in range(2):
                own = jnp.where((lane >= HD) == (head == 1), queries, jnp.zeros_like(queries))
                scores = jnp.where(key_slot < length, product(keys, own, NT), -1e30)
                top = jnp.max(scores, axis=0, keepdims=True)
                exponent = jnp.exp(scores - top)
                total = jnp.sum(exponent, axis=0, keepdims=True)
                mixed = product(values, exponent.astype(BF), TN)
                parts.append(mixed[head * HD : (head + 1) * HD] * (1.0 / total))
                lse_ref[pl.ds(pair * 2 + head, 1), rows_at] = top + jnp.log(total)
            o_ref[rows_at, cols] = jnp.concatenate(parts, axis=0).T.astype(BF)
        return carry

    lax.fori_loop(0, rows // block, attend, 0)


def attend_forward(lengths, x, wq, wk, wv, bq, bv, block):
    rows, width = x.shape[0], wq.shape[1]
    vmem = pl.BlockSpec(memory_space=pltpu.VMEM)
    out = jax.ShapeDtypeStruct((rows, width), BF)
    return pl.pallas_call(
        functools.partial(attend_forward_kernel, block),
        in_specs=[pl.BlockSpec(memory_space=pltpu.SMEM)] + [vmem] * 6,
        out_specs=[vmem] * 5,
        out_shape=[out, out, out, out, jax.ShapeDtypeStruct((8, rows), F32)],
        compiler_params=pltpu.CompilerParams(vmem_limit_bytes=56 << 20),
        cost_estimate=pl.CostEstimate(
            flops=20 * 10**9, bytes_accessed=12 << 20, transcendentals=8 << 20
        ),
        name="attend_forward",
    )(lengths, x, wq, wk, wv, bq.reshape(1, -1), bv.reshape(1, -1))


def attend_backward_kernel(
    block,
    len_ref,
    q_ref,
    k_ref,
    v_ref,
    o_ref,
    do_ref,
    lse_ref,
    dq_ref,
    dk_ref,
    dv_ref,
    key_sum,
    value_sum,
):
    rows, width = q_ref.shape
    blocks_per_seq = LEN // block

    def back(index, carry):
        seq = index // blocks_per_seq
        keys_at = pl.ds(pl.multiple_of(seq * LEN, LEN), LEN)
        rows_at = pl.ds(pl.multiple_of(index * block, block), block)
        length = len_ref[seq]
        key_slot = lax.broadcasted_iota(jnp.int32, (LEN, block), 0)
        lane = lax.broadcasted_iota(jnp.int32, (block, PAIR), 1)
        starts = lax.rem(index, blocks_per_seq) == 0
        for pair in range(width // PAIR):
            cols = slice(pair * PAIR, (pair + 1) * PAIR)
            keys, values, queries = k_ref[keys_at, cols], v_ref[keys_at, cols], q_ref[rows_at, cols]
            d_out = do_ref[rows_at, cols]
            inner_all = (d_out.astype(F32) * o_ref[rows_at, cols].astype(F32)).T
            value_part, key_part, query_parts = None, None, []
            for head in range(2):
                mine = (lane >= HD) == (head == 1)
                own_q = jnp.where(mine, queries, jnp.zeros_like(queries))
                own_d = jnp.where(mine, d_out, jnp.zeros_like(d_out))
                inner = jnp.sum(inner_all[head * HD : (head + 1) * HD], axis=0, keepdims=True)
                scores = jnp.where(key_slot < length, product(keys, own_q, NT), -1e30)
                probs = jnp.exp(scores - lse_ref[pl.ds(pair * 2 + head, 1), rows_at])
                d_probs = product(values, own_d, NT)
                d_scores = (probs * (d_probs - inner) * HD ** (-0.5)).astype(BF)
                d_values = product(probs.astype(BF), own_d)
                d_keys = product(d_scores, own_q)
                value_part = d_values if head == 0 else value_part + d_values
                key_part = d_keys if head == 0 else key_part + d_keys
                query_parts.append(product(keys, d_scores, TN)[head * HD : (head + 1) * HD])
            key_part = key_part * HD**0.5
            dq_ref[rows_at, cols] = jnp.concatenate(query_parts, axis=0).T.astype(BF)

            @pl.when(starts)
            def _():
                key_sum[:, cols] = key_part
                value_sum[:, cols] = value_part

            @pl.when(jnp.logical_not(starts))
            def _():
                key_sum[:, cols] += key_part
                value_sum[:, cols] += value_part

        @pl.when(lax.rem(index, blocks_per_seq) == blocks_per_seq - 1)
        def _():
            dk_ref[keys_at, :] = key_sum[...].astype(BF)
            dv_ref[keys_at, :] = value_sum[...].astype(BF)

        return carry

    lax.fori_loop(0, rows // block, back, 0)


def attend_backward(lengths, q, k, v, o, d_out, lse, block):
    vmem = pl.BlockSpec(memory_space=pltpu.VMEM)
    out = jax.ShapeDtypeStruct(q.shape, BF)
    return pl.pallas_call(
        functools.partial(attend_backward_kernel, block),
        in_specs=[pl.BlockSpec(memory_space=pltpu.SMEM)] + [vmem] * 6,
        out_specs=[vmem] * 3,
        out_shape=[out] * 3,
        scratch_shapes=[pltpu.VMEM((LEN, q.shape[1]), F32)] * 2,
        compiler_params=pltpu.CompilerParams(vmem_limit_bytes=56 << 20),
        cost_estimate=pl.CostEstimate(
            flops=24 * 10**9, bytes_accessed=12 << 20, transcendentals=8 << 20
        ),
        name="attend_backward",
    )(lengths, q, k, v, o, d_out, lse)


def norm_forward(values, gain, bias):
    center = values - jnp.mean(values, axis=-1, keepdims=True)
    inverse = lax.rsqrt(jnp.mean(center * center, axis=-1, keepdims=True) + 1e-05)
    normal = center * inverse
    return (normal * gain + bias, normal, inverse)


def norm_backward(grad, normal, inverse, gain):
    scaled = grad * gain
    first_mean = jnp.mean(scaled, axis=-1, keepdims=True)
    second_mean = jnp.mean(scaled * normal, axis=-1, keepdims=True)
    return (
        inverse * (scaled - first_mean - normal * second_mean),
        jnp.sum(grad * normal, 0),
        jnp.sum(grad, 0),
    )


def exact_gelu(values):
    return jax.nn.gelu(values, approximate=False)


GROUP = 8


def dp_groups():
    size = lax.axis_size("dp")
    return [list(range(first, first + GROUP)) for first in range(0, size, GROUP)]


def gather_weights(packed):
    rows = packed.shape[0]
    own = lax.rem(lax.axis_index("dp"), GROUP)
    piece = lax.dynamic_slice_in_dim(packed, own * (rows // GROUP), rows // GROUP, 0)
    along = lax.all_gather(piece, "tensor", axis=0, tiled=False)
    full = lax.all_gather(along, "dp", axis=1, tiled=False, axis_index_groups=dp_groups())
    return full.reshape(along.shape[0], rows, packed.shape[1])


def reduce_grads(packed):
    tensor_size, rows, cols = packed.shape
    part = lax.psum_scatter(
        packed.reshape(tensor_size, GROUP, rows // GROUP, cols),
        "dp",
        scatter_dimension=1,
        axis_index_groups=dp_groups(),
        tiled=False,
    )
    part = lax.psum_scatter(part, "tensor", scatter_dimension=0, tiled=False)
    full = lax.all_gather(part, "dp", axis=0, tiled=True, axis_index_groups=dp_groups()).astype(F32)
    if lax.axis_size("dp") > GROUP:
        full = lax.psum(
            full,
            "dp",
            axis_index_groups=[
                list(range(first, lax.axis_size("dp"), GROUP)) for first in range(GROUP)
            ],
        )
    return full


def on_device(
    inputs,
    cotangent,
    lengths,
    query_weight,
    key_weight,
    value_weight,
    query_bias,
    value_bias,
    out_weight,
    out_bias,
    norm1_gain,
    norm1_bias,
    up_weight,
    up_bias,
    down_weight,
    down_bias,
    norm2_gain,
    norm2_bias,
):
    tensor_size = lax.axis_size("tensor")
    tensor_pos = lax.axis_index("tensor")
    row_count, model = inputs.shape
    share_rows = row_count // tensor_size
    first_share = tensor_pos * share_rows
    width = out_weight.shape[0]
    hidden_width = down_weight.shape[0]

    packed = jnp.concatenate([out_weight, up_weight, down_weight], axis=0)
    full = gather_weights(packed)
    out_full = full[:, :width].reshape(tensor_size * width, model)
    up_full = full[:, width : width + model]
    down_full = full[:, width + model :]

    queries, keys, values, attended, log_total = attend_forward(
        lengths, inputs, query_weight, key_weight, value_weight, query_bias, value_bias, 512
    )

    def to_rows(split_heads):
        moved = lax.all_to_all(
            split_heads.reshape(tensor_size, share_rows, -1), "tensor", 0, 0, tiled=False
        )
        return moved.transpose(1, 0, 2).reshape(share_rows, -1)

    def to_heads(split_rows):
        moved = split_rows.reshape(share_rows, tensor_size, -1).transpose(1, 0, 2)
        return lax.all_to_all(moved, "tensor", 0, 0, tiled=False).reshape(row_count, -1)

    attended_rows = to_rows(attended)
    input_share = lax.dynamic_slice_in_dim(inputs, first_share, share_rows, 0).astype(F32)
    first = input_share + product(attended_rows, out_full) + out_bias
    normed1, normal1, inverse1 = norm_forward(first, norm1_gain, norm1_bias)
    hidden_low = normed1.astype(BF)
    up_bias_full = lax.all_gather(up_bias, "tensor", axis=0, tiled=False)
    uppers, actives, mlp = [], [], 0.0
    for part in range(tensor_size):
        upper = product(hidden_low, up_full[part]) + up_bias_full[part]
        active = exact_gelu(upper).astype(BF)
        mlp = mlp + product(active, down_full[part])
        uppers.append(upper)
        actives.append(active)
    second = normed1 + mlp + down_bias
    outputs, normal2, inverse2 = norm_forward(second, norm2_gain, norm2_bias)
    row_index = first_share + jnp.arange(share_rows)
    row_length = jnp.sum(
        jnp.where(
            (row_index // LEN)[:, None] == jnp.arange(lengths.shape[0])[None, :],
            lengths[None, :],
            0,
        ),
        1,
    )
    row_valid = (row_index % LEN < row_length).astype(F32)
    grad_out = cotangent.astype(F32) * row_valid[:, None]
    d_second, norm2_gain_part, norm2_bias_part = norm_backward(
        grad_out, normal2, inverse2, norm2_gain
    )
    down_bias_part = jnp.sum(d_second, 0)
    d_second_low = d_second.astype(BF)
    d_normed1 = d_second
    up_grads, down_grads, up_bias_parts = [], [], []
    for part in range(tensor_size):
        down_grads.append(product(actives[part], d_second_low, TN).astype(BF))
        d_active = product(d_second_low, down_full[part], NT)
        d_upper = jax.vjp(exact_gelu, uppers[part])[1](d_active)[0].astype(BF)
        up_grads.append(product(hidden_low, d_upper, TN).astype(BF))
        up_bias_parts.append(jnp.sum(d_upper.astype(F32), 0))
        d_normed1 = d_normed1 + product(d_upper, up_full[part], NT)
    d_first, norm1_gain_part, norm1_bias_part = norm_backward(
        d_normed1, normal1, inverse1, norm1_gain
    )
    out_bias_part = jnp.sum(d_first, 0)
    d_first_low = d_first.astype(BF)
    out_grad = product(attended_rows, d_first_low, TN).astype(BF).reshape(tensor_size, width, model)
    d_attended = to_heads(product(d_first_low, out_full, NT).astype(BF))
    reduced = reduce_grads(
        jnp.concatenate([out_grad, jnp.stack(up_grads), jnp.stack(down_grads)], axis=1)
    )
    d_queries, d_keys, d_values = attend_backward(
        lengths, queries, keys, values, attended, d_attended, log_total, 512
    )
    total = product(d_queries, query_weight, NT)
    total = total + product(d_keys, key_weight, NT) + product(d_values, value_weight, NT)
    input_grad = (
        lax.psum_scatter(total.astype(BF), "tensor", scatter_dimension=0, tiled=True).astype(F32)
        + d_first
    )
    (
        query_weight_grad,
        key_weight_grad,
        value_weight_grad,
        query_bias_grad,
        value_bias_grad,
    ) = lax.psum(
        (
            product(inputs, d_queries, TN),
            product(inputs, d_keys, TN),
            product(inputs, d_values, TN),
            jnp.sum(d_queries.astype(F32), 0),
            jnp.sum(d_values.astype(F32), 0),
        ),
        "dp",
    )
    small = lax.psum(
        jnp.stack(
            [
                norm1_gain_part,
                norm1_bias_part,
                norm2_gain_part,
                norm2_bias_part,
                out_bias_part,
                down_bias_part,
                *up_bias_parts,
            ]
        ),
        ("dp", "tensor"),
    )
    up_bias_grad = lax.dynamic_index_in_dim(small[6:], tensor_pos, 0, keepdims=False)
    return (
        outputs.astype(BF),
        input_grad,
        query_weight_grad,
        key_weight_grad,
        value_weight_grad,
        query_bias_grad,
        value_bias_grad,
        reduced[:width],
        small[4],
        small[0],
        small[1],
        reduced[width : width + model],
        up_bias_grad,
        reduced[width + model :],
        small[5],
        small[2],
        small[3],
    )


def solution(mesh):
    rows = P(("dp", "tensor"), None)
    by_col = P(None, "tensor")
    by_row = P("tensor", None)
    split = P("tensor")
    whole = P()
    return jax.shard_map(
        on_device,
        mesh=mesh,
        in_specs=(
            P("dp", None),
            rows,
            P("dp"),
            by_col,
            by_col,
            by_col,
            split,
            split,
            by_row,
            whole,
            whole,
            whole,
            by_col,
            split,
            by_row,
            whole,
            whole,
            whole,
        ),
        out_specs=(
            rows,
            rows,
            by_col,
            by_col,
            by_col,
            split,
            split,
            by_row,
            whole,
            whole,
            whole,
            by_col,
            split,
            by_row,
            whole,
            whole,
            whole,
        ),
        check_vma=False,
    )
```

time: 1240 us -> 682 us (0.55)
  waiting for transfers between devices: 639 us -> 344 us
  matrix products: 371 us -> 101 us
  Pallas kernels: 0 us -> 52.1 us
  local copies, waits for them, and re-layouts: 75.2 us -> 30.7 us
  blocking collectives: 55.6 us -> 85 us
  other arithmetic: 57.7 us -> 40.2 us
  loops' own time: 14 us -> 0 us
    dot_general x46 -> x33, matrix products: 371 us -> 101 us  [product(): return lax.dot_general(left, right, dims, preferred_element_type=F32)]
    reduce_scatter x4 -> x3, waiting for transfers between devices: 302 us -> 195 us  [the longest x1 118 us: reduce_grads(): lax.psum_scatter(packed.reshape(tensor_size, GROUP, rows // GROUP, cols),...]
    all_gather x3, waiting for transfers between devices: 227 us -> 131 us  [the longest x1 53.6 us: gather_weights(): along = lax.all_gather(piece, 'tensor', axis=0, tiled=False)]
    psum x1, waiting for transfers between devices: 109 us -> 17.2 us  [on_device(): lax.psum((product(inputs, d_queries, TN), product(inputs, d_keys, TN), pr...]
    pallas_call x0 -> x2, Pallas kernels: none -> 52.1 us  [the longest x1 28.6 us: attend_backward(): pl.pallas_call(functools.partial(attend_backward_kernel, block), in_specs...]
    all_gather x0 -> x1, blocking collectives: none -> 31.3 us  [on_device(): up_bias_full = lax.all_gather(up_bias, 'tensor', axis=0, tiled=False)]
    dynamic_slice x36 -> x1, local copies, waits for them, and re-layouts: 29 us -> 0.61 us  [on_device(): lax.dynamic_index_in_dim(small[6:], tensor_pos, 0, keepdims=False)]
    concatenate x0 -> x2, other arithmetic: none -> 26.9 us  [the longest x1 24.5 us: on_device(): jnp.concatenate([out_grad, jnp.stack(up_grads), jnp.stack(down_grads)], a...]
  transfers between devices with their start and end apart: 8 -> 9, of which waited for: 8 -> 7; matrix products, arithmetic and copies ran while one was open for 3% -> 5% of each run, Pallas kernels for 0% -> 8%
where the time goes in v1:
time: 682 us; the launch traced here: 676 us
  waiting for transfers between devices  344 us (50%)
  matrix products  101 us (15%)
  blocking collectives  85 us (12%)
  Pallas kernels  52.1 us (8%)
  other arithmetic  40.2 us (6%)
  local copies, waits for them, and re-layouts  30.7 us (5%)
  between operations  14.9 us (2%)
  starting transfers between devices  8.66 us (1%)
    reduce_scatter x1, waiting for transfers between devices, reduce_grads(): lax.psum_scatter(packed.reshape(tensor_size, GROUP, rows // GROUP, cols),...  118 us
    dot_general x33, matrix products, product(): return lax.dot_general(left, right, dims, preferred_element_type=F32)  101 us
    reduce_scatter x1, waiting for transfers between devices, on_device(): lax.psum_scatter(total.astype(BF), 'tensor', scatter_dimension=0, tiled=T...  73.2 us
    all_gather x1, waiting for transfers between devices, gather_weights(): along = lax.all_gather(piece, 'tensor', axis=0, tiled=False)  53.6 us
    psum x1, blocking collectives, on_device(): lax.psum(jnp.stack([norm1_gain_part, norm1_bias_part, norm2_gain_part, no...  40.3 us
    all_gather x1, waiting for transfers between devices, gather_weights(): lax.all_gather(along, 'dp', axis=1, tiled=False, axis_index_groups=dp_gro...  39.2 us
    all_gather x1, waiting for transfers between devices, reduce_grads(): lax.all_gather(part, 'dp', axis=0, tiled=True, axis_index_groups=dp_group...  38.5 us
    all_gather x1, blocking collectives, on_device(): up_bias_full = lax.all_gather(up_bias, 'tensor', axis=0, tiled=False)  31.3 us
  transfers between devices with their start and end apart: 9, of which 7 were waited for; matrix products, arithmetic and copies ran while one was open for 5% of the time, Pallas kernels for 8%

profile of v1, /device:TPU:0, one launch (start us, length us, event | category | flops | bytes accessed | tf_op | source)
XLA Modules:
  0.0 676.5 jit_solution(13806779717174653726)
XLA Ops:
  9.8 53.6 %all-gather.8.cloned.1.call-done = bf16[1152,1024]{1,0:T(8,128)(2,1)} async-done(((bf16[288,1024]{1,0:T(8,128)(2,1)}), bf16[1152,1024]{1,0:T(8,128)(2,1)}) %all-gather.8.cloned.1.call-update) | async-done | bytes 2359312 | tf_op jit(solution)/shard_map/all_gather | solution.py:217
  63.4 23.5 %attend_forward.1 = (bf16[2048,256]{1,0:T(8,128)(2,1)}, bf16[2048,256]{1,0:T(8,128)(2,1)}, bf16[2048,256]{1,0:T(8,128)(2,1)}, bf16[2048,256]{1,0:T(8,128)(2,1)}, f32[8,2048]{1,0:T(8,128)}) custom-call(s32[2]{0:T(128)} %len_ref.3, bf16[2048,1024]{1,0:T(8,128)(2,1)} %x_ref.1, bf16[1024,256]{1,0:T(8,128)(2,1)} %wq_ref.1, bf16[1024,256]{1,0:T(8,128)(2,1)} %wk_ref.1, ...), custom_call_target="tpu_custom_call" | custom-call | flops 20000000000 | bytes 12582912 | tf_op jit(solution)/shard_map/attend_forward/pallas_call | solution.py:84
  86.9 3.7 all-to-all-start
  90.6 31.3 %all-gather.2 = f32[4096]{0:T(1024)S(1)} all-gather(f32[1024]{0:T(1024)S(1)} %copy-done.15), channel_id=4, replica_groups=mesh['dp'=8,'tensor'=4] {'tensor'}, dimensions={0}, use_global_device_ids=true | all-gather | bytes 20480 | tf_op jit(solution)/shard_map/all_gather | solution.py:297
  123.7 39.2 %all-gather.10.cloned.1.call-done = bf16[4,2304,1024]{2,1,0:T(8,128)(2,1)} async-done(((bf16[4,288,1024]{2,1,0:T(8,128)(2,1)}), bf16[4,2304,1024]{2,1,0:T(8,128)(2,1)}) %all-gather.10.cloned.1.call-update) | async-done | bytes 18874384 | tf_op jit(solution)/shard_map/all_gather | solution.py:218
  167.3 8.4 %multiply_convert_fusion = (bf16[512,1024]{1,0:T(8,128)(2,1)S(1)}, f32[512,1024]{1,0:T(8,128)}, f32[512,1024]{1,0:T(8,128)}) fusion(f32[1024]{0:T(1024)S(1)} %get-tuple-element.135, bf16[512,1024]{1,0:T(8,128)(2,1)S(1)} %fusion.28, bf16[4,2304,1024]{2,1,0:T(8,128)(2,1)} %all-gather.10.cloned.1.call-done), kind=kOutput, calls=%fused_computation.58 | convolution fusion | flops 1108344832 | bytes 8392704 | tf_op jit(solution)/shard_map/dot_general | solution.py:21
  175.7 7.0 %multiply_convert_fusion.1 = (bf16[512,1024]{1,0:T(8,128)(2,1)S(1)}, f32[512,1024]{1,0:T(8,128)}, f32[512,1024]{1,0:T(8,128)}) fusion(f32[1024]{0:T(1024)S(1)} %get-tuple-element.136, bf16[512,1024]{1,0:T(8,128)(2,1)S(1)} %fusion.28, bf16[4,2304,1024]{2,1,0:T(8,128)(2,1)S(1)} %bitcast.187), kind=kOutput, calls=%fused_computation.71 | convolution fusion | flops 1108344832 | bytes 8392704 | tf_op jit(solution)/shard_map/dot_general | solution.py:21
  183.9 12.7 %multiply_convert_fusion.3 = (bf16[512,1024]{1,0:T(8,128)(2,1)S(1)}, f32[512,1024]{1,0:T(8,128)S(1)}, f32[512,1024]{1,0:T(8,128)}) fusion(f32[1024]{0:T(1024)S(1)} %get-tuple-element.138, bf16[512,1024]{1,0:T(8,128)(2,1)S(1)} %fusion.28, bf16[4,2304,1024]{2,1,0:T(8,128)(2,1)S(1)} %bitcast.187), kind=kOutput, calls=%fused_computation.97 | convolution fusion | flops 1108344832 | bytes 8392704 | tf_op jit(solution)/shard_map/dot_general | solution.py:21
  198.0 7.6 %multiply_convert_fusion.2 = (bf16[512,1024]{1,0:T(8,128)(2,1)S(1)}, f32[512,1024]{1,0:T(8,128)}, f32[512,1024]{1,0:T(8,128)}) fusion(f32[1024]{0:T(1024)S(1)} %get-tuple-element.137, bf16[512,1024]{1,0:T(8,128)(2,1)S(1)} %fusion.28, bf16[4,2304,1024]{2,1,0:T(8,128)(2,1)S(1)} %bitcast.187), kind=kOutput, calls=%fused_computation.84 | convolution fusion | flops 1108344832 | bytes 8392704 | tf_op jit(solution)/shard_map/dot_general | solution.py:21
  219.3 3.6 convert_reduce_fusion
  231.0 3.8 convert_reduce_fusion.2
  250.0 3.9 multiply_reduce_fusion.1
  257.7 24.5 %maximum_maximum_fusion = bf16[4,2304,1024]{2,1,0:T(8,128)(2,1)S(1)} fusion(bf16[1,1024,1024]{2,1,0:T(8,128)(2,1)S(1)} %convert_bitcast_fusion, bf16[1,1024,1024]{2,1,0:T(8,128)(2,1)S(1)} %convert_bitcast_fusion.1, bf16[1,1024,1024]{2,1,0:T(8,128)(2,1)S(1)} %convert_bitcast_fusion.2, bf16[1,1024,1024]{2,1,0:T(8,128)(2,1)S(1)} %convert_bitcast_fusion.3, ...), kind=kLoop, calls=%fused_computation | loop fusion | flops 169869312 | bytes 37748736 | tf_op jit(solution)/shard_map/concatenate | solution.py:340
  282.2 6.7 copy.54
  292.9 4.6 all-to-all-start.1
  297.5 117.8 %reduce-scatter.6.cloned.1.call-done = bf16[4,1,288,1024]{3,2,0,1:T(8,128)(2,1)} async-done(((bf16[4,8,288,1024]{3,2,0,1:T(8,128)(2,1)}), bf16[4,1,288,1024]{3,2,0,1:T(8,128)(2,1)}) %reduce-scatter.6.cloned.1.call-update) | async-done | bytes 2359312 | tf_op jit(solution)/shard_map/reduce_scatter | solution.py:224
  416.3 28.6 %attend_backward.1 = (bf16[2048,256]{1,0:T(8,128)(2,1)}, bf16[2048,256]{1,0:T(8,128)(2,1)}, bf16[2048,256]{1,0:T(8,128)(2,1)}) custom-call(s32[2]{0:T(128)} %len_ref.3, bf16[2048,256]{1,0:T(8,128)(2,1)} %get-tuple-element.26.q_ref, bf16[2048,256]{1,0:T(8,128)(2,1)} %get-tuple-element.27.k_ref, bf16[2048,256]{1,0:T(8,128)(2,1)} %get-tuple-element.28.v_ref, ...), custom_call_target="tpu_custom_call" | custom-call | flops 24000000000 | bytes 12582912 | tf_op jit(solution)/shard_map/attend_backward/pallas_call | solution.py:169
  461.4 4.1 reduce-scatter.8.cloned.1.call-done
  465.6 40.3 %psum.47 = f32[10,1024]{1,0:T(8,128)S(1)} all-reduce(f32[10,1024]{1,0:T(8,128)S(1)} %stack.83), channel_id=1, replica_groups=mesh['dp'=8,'tensor'=4] {'dp','tensor'}, use_global_device_ids=true, to_apply=%region_29.30 | all-reduce | flops 10240 | bytes 81920 | tf_op jit(solution)/shard_map/psum | solution.py:367
  508.9 13.5 %all-reduce = (f32[256]{0:T(256)}, f32[256]{0:T(256)}) all-reduce(f32[256]{0:T(256)S(1)} %convert_reduce_fusion.5, f32[256]{0:T(256)S(1)} %convert_reduce_fusion.4), channel_id=1, replica_groups=mesh['dp'=8,'tensor'=4] {'dp'}, use_global_device_ids=true, to_apply=%region_14.15 | all-reduce | flops 512 | bytes 4096 | tf_op jit(solution)/shard_map/psum | solution.py:357
  522.4 17.2 %all-reduce.4.cloned.1.call-done = (f32[1024,256]{0,1:T(8,128)}, f32[1024,256]{0,1:T(8,128)}, f32[1024,256]{0,1:T(8,128)}) async-done(((f32[1024,256]{0,1:T(8,128)}, f32[1024,256]{0,1:T(8,128)}, f32[1024,256]{0,1:T(8,128)}), (f32[1024,256]{0,1:T(8,128)}, f32[1024,256]{0,1:T(8,128)}, f32[1024,256]{0,1:T(8,128)})) %all-reduce.4.cloned.1.call-update) | async-done | bytes 3145744 | tf_op jit(solution)/shard_map/psum | solution.py:357
  546.1 73.2 %reduce-scatter.4.cloned.1.call-done = bf16[512,1024]{1,0:T(8,128)(2,1)} async-done(((bf16[2048,1024]{1,0:T(8,128)(2,1)}), bf16[512,1024]{1,0:T(8,128)(2,1)}) %reduce-scatter.4.cloned.1.call-update) | async-done | bytes 1048592 | tf_op jit(solution)/shard_map/reduce_scatter | solution.py:348
  622.1 38.5 %all-gather.12.cloned.1.call-done = bf16[1,2304,1024]{2,1,0:T(8,128)(2,1)} async-done(((bf16[1,288,1024]{2,1,0:T(8,128)(2,1)}), bf16[1,2304,1024]{2,1,0:T(8,128)(2,1)}) %all-gather.12.cloned.1.call-update) | async-done | bytes 4718608 | tf_op jit(solution)/shard_map/all_gather | solution.py:232
  665.2 4.2 slice_bitcast_fusion
  (142 shorter events, 90.1 us)
Async XLA Ops:
  7.2 56.2 %all-gather.8.cloned.1.call-start = ((), (), s32[]{:S(2)}) async-start(), calls=%async_computation.8 | async-start | bytes 2949120 | tf_op jit(solution)/shard_map/all_gather | solution.py:217
  9.7 153.2 %all-gather.10.cloned.1.call-start = ((), (), s32[]{:S(2)}) async-start(), calls=%async_computation.9 | async-start | bytes 21233664 | tf_op jit(solution)/shard_map/all_gather | solution.py:218
  86.9 3.7 copy-start.15
  86.9 35.0 %copy-start.16 = (s32[2]{0:T(128)S(1)}, s32[2]{0:T(128)}, u32[]{:S(2)}) copy-start(s32[2]{0:T(128)} %len_ref.3) | copy-start | bytes 28
  86.9 76.0 %copy-start.18 = (f32[1024]{0:T(1024)S(1)}, f32[1024]{0:T(1024)}, u32[]{:S(2)}) copy-start(f32[1024]{0:T(1024)} %param.27) | copy-start | bytes 12292
  86.9 35.1 %all-to-all-start = ((bf16[4,512,256]{2,1,0:T(8,128)(2,1)}), bf16[4,512,256]{2,1,0:T(8,128)(2,1)S(1)}, u32[]{:S(2)}, u32[]{:S(2)}) async-start(bf16[4,512,256]{2,1,0:T(8,128)(2,1)} %bitcast.189), calls=%async_computation | async-start | bytes 2097152 | tf_op jit(solution)/shard_map/all_to_all | solution.py:283
  90.6 324.7 %reduce-scatter.6.cloned.1.call-start = ((), (), s32[]{:S(2)}) async-start(), calls=%async_computation.6 | async-start | bytes 21233664 | tf_op jit(solution)/shard_map/reduce_scatter | solution.py:224
  166.8 8.8 %slice-start = ((s8[18874368]{0:T(1024)(128)(4,1)}), s8[4194304]{0:T(1024)(128)(4,1)S(1)}, s32[]{:S(2)}) async-start(s8[18874368]{0:T(1024)(128)(4,1)} %bitcast.186), calls=%async_computation.12 | async-start | bytes 8388608
  167.2 8.4 %slice-start.1 = ((s8[18874368]{0:T(1024)(128)(4,1)}), s8[4194304]{0:T(1024)(128)(4,1)S(1)}, s32[]{:S(2)}) async-start(s8[18874368]{0:T(1024)(128)(4,1)} %bitcast.186), calls=%async_computation.13 | async-start | bytes 8388608
  167.2 8.4 %slice-start.2 = ((s8[18874368]{0:T(1024)(128)(4,1)}), s8[4194304]{0:T(1024)(128)(4,1)S(1)}, s32[]{:S(2)}) async-start(s8[18874368]{0:T(1024)(128)(4,1)} %bitcast.186), calls=%async_computation.14 | async-start | bytes 8388608
  167.2 8.4 %slice-start.3 = ((s8[18874368]{0:T(1024)(128)(4,1)}), s8[4194304]{0:T(1024)(128)(4,1)S(1)}, s32[]{:S(2)}) async-start(s8[18874368]{0:T(1024)(128)(4,1)} %bitcast.186), calls=%async_computation.15 | async-start | bytes 8388608
  167.3 8.4 %slice-start.4 = ((s8[18874368]{0:T(1024)(128)(4,1)}), s8[2097152]{0:T(1024)(128)(4,1)S(1)}, s32[]{:S(2)}) async-start(s8[18874368]{0:T(1024)(128)(4,1)} %bitcast.186), calls=%async_computation.16 | async-start | bytes 4194304
  217.1 2.2 copy-start.26
  292.9 122.4 %all-to-all-start.1 = ((bf16[4,512,256]{2,1,0:T(8,128)(2,1)}), bf16[4,512,256]{2,1,0:T(8,128)(2,1)S(1)}, u32[]{:S(2)}, u32[]{:S(2)}) async-start(bf16[4,512,256]{2,1,0:T(8,128)(2,1)} %bitcast.180), calls=%async_computation.1 | async-start | bytes 2097152 | tf_op jit(solution)/shard_map/all_to_all | solution.py:290
  297.5 168.0 %reduce-scatter.8.cloned.1.call-start = ((), (), s32[]{:S(2)}) async-start(), calls=%async_computation.7 | async-start | bytes 2949120 | tf_op jit(solution)/shard_map/reduce_scatter | solution.py:231
  415.3 124.3 %all-reduce.4.cloned.1.call-start = ((), (), s32[]{:S(2)}) async-start(), calls=%async_computation.11 | async-start | bytes 6291456 | tf_op jit(solution)/shard_map/psum | solution.py:357
  416.3 28.6 %copy-start.17 = (bf16[2048,1024]{1,0:T(8,128)(2,1)S(1)}, bf16[2048,1024]{1,0:T(8,128)(2,1)}, u32[]{:S(2)}) copy-start(bf16[2048,1024]{1,0:T(8,128)(2,1)} %x_ref.1) | copy-start | bytes 12582916
  444.9 3.6 copy-start.4
  448.5 2.2 copy-start.2
  453.0 166.3 %reduce-scatter.4.cloned.1.call-start = ((), (), s32[]{:S(2)}) async-start(), calls=%async_computation.5 | async-start | bytes 5242880 | tf_op jit(solution)/shard_map/reduce_scatter | solution.py:348
  454.2 2.5 copy-start.5
  454.2 2.5 copy-start.9
  461.3 199.3 %all-gather.12.cloned.1.call-start = ((), (), s32[]{:S(2)}) async-start(), calls=%async_computation.10 | async-start | bytes 5308416 | tf_op jit(solution)/shard_map/all_gather | solution.py:232
  539.6 5.2 copy-start.7
  (18 other events, 25.5 us)
Sparse Core Ops, SparseCore 0:
  10.2 53.1 all-gather.7
  65.3 97.5 all-gather.9
  289.1 126.1 reduce-scatter.5
  417.4 48.0 reduce-scatter.7
  469.5 70.0 all-reduce.3
  542.4 76.8 reduce-scatter.3
  621.2 39.4 all-gather.11

commit v2 on v1

v2 whole, which is shorter than its diff:
```python
import functools

import jax
import jax.numpy as jnp
from jax import lax
from jax.experimental import pallas as pl
from jax.experimental.pallas import tpu as pltpu
from jax.sharding import PartitionSpec as P

HD = 64
LEN = 1024
PAIR = 2 * HD
GROUP = 8
F32 = jnp.float32
BF = jnp.bfloat16
NN = (((1,), (0,)), ((), ()))
NT = (((1,), (1,)), ((), ()))
TN = (((0,), (0,)), ((), ()))
MESH = pl.DeviceIdType.MESH
VMEM_LIMIT = 60 << 20


def product(left, right, dims=NN):
    return lax.dot_general(left, right, dims, preferred_element_type=F32)


def flip(index, bit):
    return index + bit * (1 - 2 * lax.rem(lax.div(index, bit), 2))


def mix(index, step):
    low = lax.rem(index + step, 2)
    high = lax.rem(lax.div(index, 2) + lax.div(step, 2), 2)
    return 2 * high + low


class Place:
    def __init__(self):
        self.dp = lax.axis_index("dp")
        self.t = lax.axis_index("tensor")
        self.e = lax.rem(self.dp, GROUP)
        self.core = lax.rem(self.e, 2)
        self.quad = lax.div(self.e, 2)
        self.to_core = (flip(self.dp, 1), self.t)
        self.to_x = (flip(self.dp, 2), self.t)
        self.to_y = (flip(self.dp, 4), self.t)
        self.quad_x = flip(self.quad, 1)
        self.quad_y = flip(self.quad, 2)
        self.quad_xy = flip(self.quad_x, 2)

    def to_z(self, step):
        return (self.dp, mix(self.t, jnp.int32(step)))

    def greet(self):
        barrier = pltpu.get_barrier_semaphore()
        peers = [self.to_core, self.to_x, self.to_y, self.to_z(1), self.to_z(2), self.to_z(3)]
        for peer in peers:
            pl.semaphore_signal(barrier, inc=1, device_id=peer, device_id_type=MESH)
        pl.semaphore_wait(barrier, len(peers))


def remote(src, dst, send, recv, index, device):
    return pltpu.make_async_remote_copy(
        src_ref=src,
        dst_ref=dst,
        send_sem=send.at[index],
        recv_sem=recv.at[index],
        device_id=device,
        device_id_type=MESH,
    )


class Spread:
    def __init__(self, place, full, sems, index):
        self.p = place
        self.full = full
        self.sems = sems
        self.index = index

    def block(self, step):
        return mix(self.p.t, jnp.int32(step)) if step else self.p.t

    def slot(self, step):
        return self.index * 4 + step

    def x_copy(self, step):
        p = self.p
        ref = self.full.at[self.block(step), p.quad, p.core]
        return remote(ref, ref, self.sems[0], self.sems[1], self.slot(step), p.to_x)

    def y_copy(self, step):
        p = self.p
        ref = self.full.at[self.block(step), p.quad, p.core]
        return remote(ref, ref, self.sems[2], self.sems[3], self.slot(step), p.to_y)

    def half_copies(self, step):
        p = self.p
        half = self.full.shape[3] // 2
        first = self.full.at[self.block(step), p.quad_x, p.core, pl.ds(0, half)]
        second = self.full.at[self.block(step), p.quad_y, p.core, pl.ds(half, half)]
        return (
            remote(first, first, self.sems[4], self.sems[5], self.slot(step), p.to_y),
            remote(second, second, self.sems[6], self.sems[7], self.slot(step), p.to_x),
        )

    def core_copy(self, step):
        p = self.p
        ref = self.full.at[self.block(step), :, p.core]
        return remote(ref, ref, self.sems[8], self.sems[9], self.slot(step), p.to_core)

    def first(self, step):
        self.x_copy(step).start()
        self.y_copy(step).start()

    def second(self, step):
        self.x_copy(step).wait_recv()
        self.y_copy(step).wait_recv()
        for copy in self.half_copies(step):
            copy.start()

    def third(self, step):
        for copy in self.half_copies(step):
            copy.wait_recv()
        self.core_copy(step).start()

    def arrived(self, step):
        self.core_copy(step).wait_recv()

    def finish(self, step):
        self.x_copy(step).wait_send()
        self.y_copy(step).wait_send()
        for copy in self.half_copies(step):
            copy.wait_send()
        self.core_copy(step).wait_send()

    @staticmethod
    def scratch(count):
        return [pltpu.SemaphoreType.DMA((4 * count,))] * 10


def norm_center(values):
    center = values - jnp.mean(values, axis=-1, keepdims=True)
    inverse = lax.rsqrt(jnp.mean(center * center, axis=-1, keepdims=True) + 1e-05)
    return center * inverse, inverse


def norm_back(grad, normal, inverse, gain):
    scaled = grad * gain
    first_mean = jnp.mean(scaled, axis=-1, keepdims=True)
    second_mean = jnp.mean(scaled * normal, axis=-1, keepdims=True)
    return inverse * (scaled - first_mean - normal * second_mean)


def forward_kernel(
    len_ref,
    x_hbm,
    cot_ref,
    vec_ref,
    small_ref,
    wq_hbm,
    wk_hbm,
    wv_hbm,
    wo_hbm,
    wu_hbm,
    wd_hbm,
    qkv_full,
    out_full,
    up_full,
    down_full,
    q_hbm,
    k_hbm,
    v_hbm,
    o_hbm,
    act_hbm,
    slope_hbm,
    outputs_ref,
    d_second_ref,
    normal1_ref,
    inverse1_ref,
    hidden_ref,
    lse_ref,
    sums_ref,
    x_seq,
    small_all,
    w_qkv,
    w_out,
    w_up,
    w_down,
    q_s,
    k_s,
    v_s,
    o_s,
    act_s,
    slope_s,
    acc,
    z_send,
    z_recv,
    small_send,
    small_recv,
    local,
    load,
    save,
    *spread_sems,
):
    p = Place()
    rows, model = acc.shape
    width = q_s.shape[2]
    half_index = lax.rem(p.t, 2)
    seq = lax.div(p.t, 2)
    own_rows = pl.ds(pl.multiple_of(half_index * rows, rows), rows)
    fulls = [qkv_full, out_full, up_full, down_full]
    spreads = [Spread(p, full, spread_sems, i) for i, full in enumerate(fulls)]
    QKV, OUT, UP, DOWN = range(4)

    own = [(w_qkv.at[0], None), (w_out.at[0], wo_hbm), (w_up.at[0], wu_hbm), (w_down.at[0], wd_hbm)]
    x_load = pltpu.make_async_copy(
        x_hbm.at[pl.ds(pl.multiple_of(seq * LEN, LEN), LEN)], x_seq, local.at[0]
    )
    own_loads = [
        pltpu.make_async_copy(w, w_qkv.at[0, :, :, :, pl.ds(i * width, width)], local.at[1 + i])
        for i, w in enumerate((wq_hbm, wk_hbm, wv_hbm))
    ]
    x_load.start()
    for copy in own_loads:
        copy.start()
    out_loads = [pltpu.make_async_copy(wo_hbm, w_out.at[0], local.at[4])]
    up_load = pltpu.make_async_copy(wu_hbm, w_up.at[0], local.at[5])
    down_load = pltpu.make_async_copy(wd_hbm, w_down.at[0], local.at[6])
    own_saves = [
        pltpu.make_async_copy(w_qkv.at[0], qkv_full.at[p.t], local.at[7]),
        pltpu.make_async_copy(wo_hbm, out_full.at[p.t], local.at[8]),
        pltpu.make_async_copy(wu_hbm, up_full.at[p.t], local.at[9]),
        pltpu.make_async_copy(wd_hbm, down_full.at[p.t], local.at[10]),
    ]

    p.greet()

    def z_copies(array, step):
        slot = array * 4 + step
        if array == QKV:
            return [
                remote(
                    w.at[p.quad, p.core],
                    qkv_full.at[p.t, p.quad, p.core, :, pl.ds(i * width, width)],
                    z_send,
                    z_recv,
                    slot if i == 0 else 16 + 4 * (i - 1) + step,
                    p.to_z(step),
                )
                for i, w in enumerate((wq_hbm, wk_hbm, wv_hbm))
            ]
        w = (None, wo_hbm, wu_hbm, wd_hbm)[array]
        return [
            remote(
                w.at[p.quad, p.core],
                fulls[array].at[p.t, p.quad, p.core],
                z_send,
                z_recv,
                slot,
                p.to_z(step),
            )
        ]

    def small_copy(step):
        return remote(
            small_ref, small_all.at[p.t], small_send, small_recv, step, p.to_z(step)
        )

    def z_start(array, step):
        for copy in z_copies(array, step):
            copy.start()

    def z_sent(array, step):
        for copy in z_copies(array, step):
            copy.wait_send()

    def z_first(array, step):
        for copy in z_copies(array, step):
            copy.wait_recv()
        spreads[array].first(step)

    small_all[p.t] = small_ref[...]
    for step in (1, 2, 3):
        small_copy(step).start()
    for step in (1, 2, 3):
        z_start(QKV, step)
    for step in (1, 2, 3):
        z_start(OUT, step)

    def load_copy(array, step, slot):
        vmem = (w_qkv, w_out, w_up, w_down)[array]
        return pltpu.make_async_copy(
            fulls[array].at[mix(p.t, jnp.int32(step))], vmem.at[slot], load.at[array * 4 + step]
        )

    def attend(step):
        group = mix(p.t, step)
        slot = lax.rem(step, 2)
        weights = w_qkv[slot].reshape(model, 3 * width)
        bias = small_all[group, 0:1]
        x_own = x_seq[own_rows, :]
        queries = (product(x_own, weights[:, :width]) + bias[:, :width]).astype(BF)
        q_s[step] = (queries.astype(F32) * HD ** (-0.5)).astype(BF)
        k_s[step] = product(x_seq[...], weights[:, width : 2 * width]).astype(BF)
        v_s[step] = (
            product(x_seq[...], weights[:, 2 * width :]) + bias[:, width : 2 * width]
        ).astype(BF)
        length = len_ref[seq]
        key_slot = lax.broadcasted_iota(jnp.int32, (LEN, rows), 0)
        lane = lax.broadcasted_iota(jnp.int32, (rows, PAIR), 1)
        for pair in range(width // PAIR):
            cols = slice(pair * PAIR, (pair + 1) * PAIR)
            keys, values, q_pair = k_s[step, :, cols], v_s[step, :, cols], q_s[step, :, cols]
            parts = []
            for head in range(2):
                mine = jnp.where((lane >= HD) == (head == 1), q_pair, jnp.zeros_like(q_pair))
                scores = jnp.where(key_slot < length, product(keys, mine, NT), -1e30)
                top = jnp.max(scores, axis=0, keepdims=True)
                exponent = jnp.exp(scores - top)
                total = jnp.sum(exponent, axis=0, keepdims=True)
                mixed = product(values, exponent.astype(BF), TN)
                parts.append(mixed[head * HD : (head + 1) * HD] * (1.0 / total))
                lse_ref[group, pl.ds(pair * 2 + head, 1), :] = top + jnp.log(total)
            o_s[step, :, cols] = jnp.concatenate(parts, axis=0).T.astype(BF)

    def attend_saves(step):
        group = mix(p.t, jnp.int32(step))
        pairs = ((q_s, q_hbm), (k_s, k_hbm), (v_s, v_hbm), (o_s, o_hbm))
        return [
            pltpu.make_async_copy(vmem.at[step], hbm.at[group], save.at[4 * step + i])
            for i, (vmem, hbm) in enumerate(pairs)
        ]

    def on(step, at, action):
        @pl.when(step == at)
        def _():
            action()

    x_load.wait()
    for copy in own_loads:
        copy.wait()
    for copy in own_saves:
        copy.start()
    out_loads[0].start()
    up_load.start()
    down_load.start()
    for step in (1, 2, 3):
        small_copy(step).wait_recv()

    def after_first():
        z_first(QKV, 1)
        z_start(UP, 1)
        spreads[QKV].second(1)
        spreads[QKV].third(1)
        spreads[QKV].arrived(1)
        load_copy(QKV, 1, 1).start()
        for step in (2, 3):
            z_first(QKV, step)
        load_copy(QKV, 1, 1).wait()

    def after_second():
        for step in (2, 3):
            z_start(UP, step)
        own_saves[0].wait()
        for step in (2, 3):
            spreads[QKV].second(step)
        for step in (1, 2, 3):
            z_first(OUT, step)
        for step in (2, 3):
            spreads[QKV].third(step)
        spreads[QKV].arrived(2)
        load_copy(QKV, 2, 0).start()
        z_first(UP, 1)
        load_copy(QKV, 2, 0).wait()

    def after_third():
        spreads[QKV].arrived(3)
        load_copy(QKV, 3, 1).start()
        for step in (1, 2, 3):
            spreads[OUT].second(step)
        spreads[UP].second(1)
        for step in (2, 3):
            z_first(UP, step)
        z_start(DOWN, 1)
        z_start(DOWN, 2)
        for step in (1, 2, 3):
            spreads[OUT].third(step)
        spreads[UP].third(1)
        load_copy(QKV, 3, 1).wait()

    def after_fourth():
        for step in (1, 2, 3):
            spreads[OUT].arrived(step)
            load_copy(OUT, step, step).start()
        spreads[UP].arrived(1)
        load_copy(UP, 1, 1).start()
        for step in (2, 3):
            spreads[UP].second(step)
        z_start(DOWN, 3)

    def attend_step(step, carry):
        attend(step)
        for i in range(4):
            on(step, i, lambda i=i: [copy.start() for copy in attend_saves(i)])
        on(step, 0, after_first)
        on(step, 1, after_second)
        on(step, 2, after_third)
        on(step, 3, after_fourth)
        return carry

    lax.fori_loop(0, 4, attend_step, 0)

    out_loads[0].wait()
    for step in (1, 2, 3):
        load_copy(OUT, step, step).wait()
    total = x_seq[own_rows, :].astype(F32) + vec_ref[0:1]
    for step in range(4):
        total = total + product(o_s[step], w_out[step].reshape(width, model))
    normal1, inverse1 = norm_center(total)
    normal1_ref[...] = normal1
    inverse1_ref[...] = jnp.broadcast_to(inverse1, inverse1_ref.shape)
    normed1 = normal1 * vec_ref[1:2] + vec_ref[2:3]
    hidden_ref[...] = normed1.astype(BF)
    acc[...] = normed1 + vec_ref[3:4]
    for step in (2, 3):
        spreads[UP].third(step)
    z_first(DOWN, 1)

    def mlp_saves(step):
        part = mix(p.t, jnp.int32(step))
        return [
            pltpu.make_async_copy(act_s.at[step], act_hbm.at[part], save.at[16 + 2 * step]),
            pltpu.make_async_copy(slope_s.at[step], slope_hbm.at[part], save.at[17 + 2 * step]),
        ]

    def up_step(step, carry):
        slot = lax.rem(step, 2)
        on(step, 0, up_load.wait)
        on(step, 1, load_copy(UP, 1, 1).wait)
        on(step, 2, load_copy(UP, 2, 0).wait)
        on(step, 3, load_copy(UP, 3, 1).wait)
        weights = w_up[slot].reshape(model, model)
        upper = product(hidden_ref[...], weights) + small_all[mix(p.t, step), 1:2]
        cdf = 0.5 * (1.0 + lax.erf(upper * 0.7071067811865476))
        act_s[step] = (upper * cdf).astype(BF)
        density = jnp.exp(-0.5 * upper * upper) * 0.3989422804014327
        slope_s[step] = (cdf + upper * density).astype(BF)
        for i in range(4):
            on(step, i, lambda i=i: [copy.start() for copy in mlp_saves(i)])

        def zero():
            spreads[UP].arrived(2)
            load_copy(UP, 2, 0).start()
            spreads[UP].arrived(3)
            spreads[DOWN].second(1)
            z_first(DOWN, 2)

        def one():
            load_copy(UP, 3, 1).start()
            spreads[DOWN].third(1)
            z_first(DOWN, 3)
            spreads[DOWN].second(2)

        def two():
            spreads[DOWN].arrived(1)
            load_copy(DOWN, 1, 1).start()
            spreads[DOWN].third(2)

        def three():
            spreads[DOWN].second(3)

        on(step, 0, zero)
        on(step, 1, one)
        on(step, 2, two)
        on(step, 3, three)
        return carry

    lax.fori_loop(0, 4, up_step, 0)

    def down_step(step, carry):
        slot = lax.rem(step, 2)
        on(step, 0, down_load.wait)
        on(step, 1, load_copy(DOWN, 1, 1).wait)
        on(step, 2, load_copy(DOWN, 2, 0).wait)
        on(step, 3, load_copy(DOWN, 3, 1).wait)
        acc[...] += product(act_s[step], w_down[slot].reshape(model, model))

        def zero():
            spreads[DOWN].arrived(2)
            load_copy(DOWN, 2, 0).start()

        def one():
            spreads[DOWN].third(3)
            spreads[DOWN].arrived(3)
            load_copy(DOWN, 3, 1).start()

        on(step, 0, zero)
        on(step, 1, one)
        return carry

    lax.fori_loop(0, 4, down_step, 0)

    normal2, inverse2 = norm_center(acc[...])
    outputs_ref[...] = (normal2 * vec_ref[4:5] + vec_ref[5:6]).astype(BF)
    slot_index = half_index * rows + lax.broadcasted_iota(jnp.int32, (rows, 1), 0)
    grad_out = jnp.where(slot_index < len_ref[seq], cot_ref[...].astype(F32), 0.0)
    d_second = norm_back(grad_out, normal2, inverse2, vec_ref[4:5])
    d_second_ref[...] = d_second
    sums_ref[0:1] = jnp.sum(grad_out * normal2, axis=0, keepdims=True)
    sums_ref[1:2] = jnp.sum(grad_out, axis=0, keepdims=True)
    sums_ref[2:3] = jnp.sum(d_second, axis=0, keepdims=True)
    sums_ref[3:8] = jnp.zeros((5, model), F32)

    for copy in own_saves[1:]:
        copy.wait()
    for step in range(4):
        for copy in attend_saves(step) + mlp_saves(step):
            copy.wait()
    for step in (1, 2, 3):
        small_copy(step).wait_send()
        for array in range(4):
            z_sent(array, step)
            spreads[array].finish(step)


def run_forward(lengths, x, cot, vec, small, wq, wk, wv, wo, wu, wd):
    tensor_size = lax.axis_size("tensor")
    model = x.shape[1]
    rows = x.shape[0] // tensor_size
    width = wo.shape[0]
    pieces = lambda w: w.reshape(4, 2, w.shape[0] // GROUP, w.shape[1])
    anyw = pl.BlockSpec(memory_space=pl.ANY)
    vmem = pl.BlockSpec(memory_space=pltpu.VMEM)
    smem = pl.BlockSpec(memory_space=pltpu.SMEM)
    T = tensor_size
    out = lambda shape, dtype=BF: jax.ShapeDtypeStruct(shape, dtype)
    outs = [
        (out((T, 4, 2, model // GROUP, 3 * width)), anyw),
        (out((T, 4, 2, width // GROUP, model)), anyw),
        (out((T, 4, 2, model // GROUP, wu.shape[1])), anyw),
        (out((T, 4, 2, wd.shape[0] // GROUP, model)), anyw),
        (out((T, rows, width)), anyw),
        (out((T, LEN, width)), anyw),
        (out((T, LEN, width)), anyw),
        (out((T, rows, width)), anyw),
        (out((T, rows, wu.shape[1])), anyw),
        (out((T, rows, wu.shape[1])), anyw),
        (out((rows, model)), vmem),
        (out((rows, model), F32), vmem),
        (out((rows, model), F32), vmem),
        (out((rows, 128), F32), vmem),
        (out((rows, model)), vmem),
        (out((T, 8, rows), F32), vmem),
        (out((8, model), F32), vmem),
    ]
    scratch = [
        pltpu.VMEM((LEN, model), BF),
        pltpu.VMEM((T, 8, model), F32),
        pltpu.VMEM((2, 4, 2, model // GROUP, 3 * width), BF),
        pltpu.VMEM((T, 4, 2, width // GROUP, model), BF),
        pltpu.VMEM((2, 4, 2, model // GROUP, wu.shape[1]), BF),
        pltpu.VMEM((2, 4, 2, wd.shape[0] // GROUP, model), BF),
        pltpu.VMEM((T, rows, width), BF),
        pltpu.VMEM((T, LEN, width), BF),
        pltpu.VMEM((T, LEN, width), BF),
        pltpu.VMEM((T, rows, width), BF),
        pltpu.VMEM((T, rows, wu.shape[1]), BF),
        pltpu.VMEM((T, rows, wu.shape[1]), BF),
        pltpu.VMEM((rows, model), F32),
        pltpu.SemaphoreType.DMA((24,)),
        pltpu.SemaphoreType.DMA((24,)),
        pltpu.SemaphoreType.DMA((4,)),
        pltpu.SemaphoreType.DMA((4,)),
        pltpu.SemaphoreType.DMA((11,)),
        pltpu.SemaphoreType.DMA((16,)),
        pltpu.SemaphoreType.DMA((24,)),
        *Spread.scratch(4),
    ]
    return pl.pallas_call(
        forward_kernel,
        in_specs=[smem, anyw, vmem, vmem, vmem] + [anyw] * 6,
        out_specs=[spec for _, spec in outs],
        out_shape=[shape for shape, _ in outs],
        scratch_shapes=scratch,
        compiler_params=pltpu.CompilerParams(
            collective_id=0, has_side_effects=True, vmem_limit_bytes=VMEM_LIMIT
        ),
        cost_estimate=pl.CostEstimate(
            flops=40 * 10**9, bytes_accessed=60 << 20, transcendentals=16 << 20
        ),
        name="forward",
    )(
        lengths,
        x,
        cot,
        vec,
        small,
        pieces(wq),
        pieces(wk),
        pieces(wv),
        pieces(wo),
        pieces(wu),
        pieces(wd),
    )


def attend_back(q_ref, k_ref, v_ref, o_ref, d_ref, lse_ref, dq_ref, dk_ref, dv_ref, length):
    rows, width = q_ref.shape
    key_slot = lax.broadcasted_iota(jnp.int32, (LEN, rows), 0)
    lane = lax.broadcasted_iota(jnp.int32, (rows, PAIR), 1)
    for pair in range(width // PAIR):
        cols = slice(pair * PAIR, (pair + 1) * PAIR)
        keys, values, queries = k_ref[:, cols], v_ref[:, cols], q_ref[:, cols]
        d_out = d_ref[:, cols]
        inner_all = (d_out.astype(F32) * o_ref[:, cols].astype(F32)).T
        value_part, key_part, query_parts = None, None, []
        for head in range(2):
            mine = (lane >= HD) == (head == 1)
            own_q = jnp.where(mine, queries, jnp.zeros_like(queries))
            own_d = jnp.where(mine, d_out, jnp.zeros_like(d_out))
            inner = jnp.sum(inner_all[head * HD : (head + 1) * HD], axis=0, keepdims=True)
            scores = jnp.where(key_slot < length, product(keys, own_q, NT), -1e30)
            probs = jnp.exp(scores - lse_ref[pl.ds(pair * 2 + head, 1), :])
            d_probs = product(values, own_d, NT)
            d_scores = (probs * (d_probs - inner) * HD ** (-0.5)).astype(BF)
            d_values = product(probs.astype(BF), own_d)
            d_keys = product(d_scores, own_q)
            value_part = d_values if head == 0 else value_part + d_values
            key_part = d_keys if head == 0 else key_part + d_keys
            query_parts.append(product(keys, d_scores, TN)[head * HD : (head + 1) * HD])
        dk_ref[:, cols] = key_part * HD**0.5
        dv_ref[:, cols] = value_part
        dq_ref[:, cols] = jnp.concatenate(query_parts, axis=0).T.astype(BF)


def attend_back_kernel(len_ref, q_ref, k_ref, v_ref, o_ref, d_ref, lse_ref, dq_ref, dk_ref, dv_ref):
    seq = lax.div(lax.axis_index("tensor"), 2)
    attend_back(
        *(r.at[0] for r in (q_ref, k_ref, v_ref, o_ref, d_ref, lse_ref, dq_ref, dk_ref, dv_ref)),
        len_ref[seq],
    )


def run_attend_back(lengths, q, k, v, o, d, lse):
    spec = lambda a: pl.BlockSpec((1,) + a.shape[1:], lambda i: (i, 0, 0))
    return pl.pallas_call(
        attend_back_kernel,
        grid=(q.shape[0],),
        in_specs=[pl.BlockSpec(memory_space=pltpu.SMEM)] + [spec(a) for a in (q, k, v, o, d, lse)],
        out_specs=[spec(q), spec(k), spec(v)],
        out_shape=[
            jax.ShapeDtypeStruct(q.shape, BF),
            jax.ShapeDtypeStruct(k.shape, F32),
            jax.ShapeDtypeStruct(v.shape, F32),
        ],
        compiler_params=pltpu.CompilerParams(vmem_limit_bytes=VMEM_LIMIT),
        name="attend_back",
    )(lengths, q, k, v, o, d, lse)


def dp_groups():
    size = lax.axis_size("dp")
    return [list(range(first, first + GROUP)) for first in range(0, size, GROUP)]


def reduce_grads(packed):
    tensor_size, rows, cols = packed.shape
    part = lax.psum_scatter(
        packed.reshape(tensor_size, GROUP, rows // GROUP, cols),
        "dp",
        scatter_dimension=1,
        axis_index_groups=dp_groups(),
        tiled=False,
    )
    part = lax.psum_scatter(part, "tensor", scatter_dimension=0, tiled=False)
    full = lax.all_gather(part, "dp", axis=0, tiled=True, axis_index_groups=dp_groups()).astype(F32)
    if lax.axis_size("dp") > GROUP:
        full = lax.psum(
            full,
            "dp",
            axis_index_groups=[
                list(range(first, lax.axis_size("dp"), GROUP)) for first in range(GROUP)
            ],
        )
    return full


def on_device(
    inputs,
    cotangent,
    lengths,
    query_weight,
    key_weight,
    value_weight,
    query_bias,
    value_bias,
    out_weight,
    out_bias,
    norm1_gain,
    norm1_bias,
    up_weight,
    up_bias,
    down_weight,
    down_bias,
    norm2_gain,
    norm2_bias,
):
    T = lax.axis_size("tensor")
    t = lax.axis_index("tensor")
    row_count, model = inputs.shape
    rows = row_count // T
    width = out_weight.shape[0]
    zero_row = jnp.zeros((model,), F32)
    vec = jnp.stack(
        [out_bias, norm1_gain, norm1_bias, down_bias, norm2_gain, norm2_bias, zero_row, zero_row]
    )
    small = jnp.stack(
        [jnp.concatenate([query_bias, value_bias, zero_row[2 * width :]]), up_bias] + [zero_row] * 6
    )
    (
        qkv_full,
        out_full,
        up_full,
        down_full,
        q,
        k,
        v,
        o,
        act,
        slope,
        outputs,
        d_second,
        normal1,
        inverse1,
        hidden,
        lse,
        sums,
    ) = run_forward(
        lengths,
        inputs,
        cotangent,
        vec,
        small,
        query_weight,
        key_weight,
        value_weight,
        out_weight,
        up_weight,
        down_weight,
    )
    qkv_full = qkv_full.reshape(T, model, 3 * width)
    out_full = out_full.reshape(T, width, model)
    up_full = up_full.reshape(T, model, -1)
    down_full = down_full.reshape(T, -1, model)
    inverse1 = inverse1[:, :1]
    d2 = d_second.astype(BF)
    d_normed1 = d_second
    up_grads, down_grads, up_bias_parts = [], [], []
    for f in range(T):
        down_grads.append(product(act[f], d2, TN).astype(BF))
        d_upper = (product(d2, down_full[f], NT) * slope[f].astype(F32)).astype(BF)
        up_grads.append(product(hidden, d_upper, TN).astype(BF))
        up_bias_parts.append(jnp.sum(d_upper.astype(F32), 0))
        d_normed1 = d_normed1 + product(d_upper, up_full[f], NT)
    d_first = norm_back(d_normed1, normal1, inverse1, norm1_gain)
    d1 = d_first.astype(BF)
    out_grads = [product(o[g], d1, TN).astype(BF) for g in range(T)]
    d_att = jnp.stack([product(d1, out_full[g], NT).astype(BF) for g in range(T)])
    dq, dk, dv = run_attend_back(lengths, q, k, v, o, d_att, lse)
    half = lax.rem(t, 2)
    both = jnp.stack([dk, dv]).reshape(2, T, 2, rows, width)
    mine = lax.dynamic_index_in_dim(both, half, 2, keepdims=False)
    other = lax.dynamic_index_in_dim(both, 1 - half, 2, keepdims=False).astype(BF)
    other = lax.ppermute(other, "tensor", [(i, i ^ 1) for i in range(T)])
    dk, dv = (mine + other.astype(F32)).astype(BF)
    own_x = lax.dynamic_slice_in_dim(inputs, t * rows, rows, 0)
    d_all = jnp.concatenate([dq, dk, dv], axis=2)
    input_grad = d_first
    qkv_grads = []
    for g in range(T):
        input_grad = input_grad + product(d_all[g], qkv_full[g], NT)
        qkv_grads.append(product(own_x, d_all[g], TN).astype(BF))
    qkv_red = reduce_grads(jnp.stack(qkv_grads).reshape(T, 3 * width, model)).reshape(model, 3 * width)
    out_red = reduce_grads(jnp.stack(out_grads))
    up_red = reduce_grads(jnp.stack(up_grads))
    down_red = reduce_grads(jnp.stack(down_grads))
    bias_rows = jnp.sum(d_all.astype(F32), 1)
    bias_rows = jnp.concatenate([bias_rows, jnp.zeros((T, model - 3 * width), F32)], axis=1)
    sums2 = jnp.stack(
        [
            jnp.sum(d_normed1 * normal1, 0),
            jnp.sum(d_normed1, 0),
            jnp.sum(d_first, 0),
        ]
    )
    total = lax.psum(
        jnp.concatenate([sums[:3], sums2, jnp.stack(up_bias_parts), bias_rows]), ("dp", "tensor")
    )
    up_bias_grad = lax.dynamic_index_in_dim(total[6 : 6 + T], t, 0, keepdims=False)
    qkv_bias = lax.dynamic_index_in_dim(total[6 + T :], t, 0, keepdims=False)
    return (
        outputs,
        input_grad,
        qkv_red[:, :width],
        qkv_red[:, width : 2 * width],
        qkv_red[:, 2 * width :],
        qkv_bias[:width],
        qkv_bias[2 * width : 3 * width],
        out_red,
        total[5],
        total[3],
        total[4],
        up_red,
        up_bias_grad,
        down_red,
        total[2],
        total[0],
        total[1],
    )


def solution(mesh):
    rows = P(("dp", "tensor"), None)
    by_col = P(None, "tensor")
    by_row = P("tensor", None)
    split = P("tensor")
    whole = P()
    return jax.shard_map(
        on_device,
        mesh=mesh,
        in_specs=(
            P("dp", None),
            rows,
            P("dp"),
            by_col,
            by_col,
            by_col,
            split,
            split,
            by_row,
            whole,
            whole,
            whole,
            by_col,
            split,
            by_row,
            whole,
            whole,
            whole,
        ),
        out_specs=(
            rows,
            rows,
            by_col,
            by_col,
            by_col,
            split,
            split,
            by_row,
            whole,
            whole,
            whole,
            by_col,
            split,
            by_row,
            whole,
            whole,
            whole,
        ),
        check_vma=False,
    )
```

time: 682 us -> 826 us (1.21)
  Pallas kernels: 52.1 us -> 181 us
  waiting for transfers between devices: 344 us -> 429 us
  matrix products: 101 us -> 50.2 us
  blocking collectives: 85 us -> 50.8 us
  local copies, waits for them, and re-layouts: 30.7 us -> 49.7 us
    pallas_call x2, Pallas kernels: 52.1 us -> 181 us  [the longest x1 156 us: run_forward(): pl.pallas_call(forward_kernel, in_specs=[smem, anyw, vmem, vmem, vmem] +...]
    all_gather x2 -> x0, waiting for transfers between devices: 92.8 us -> none  [the longest x1 53.6 us: gather_weights(): along = lax.all_gather(piece, 'tensor', axis=0, tiled=False)]
    reduce_scatter x1 -> x4, waiting for transfers between devices: 4.06 us -> 82.6 us  [reduce_grads(): part = lax.psum_scatter(part, 'tensor', scatter_dimension=0, tiled=False)]
    unnamed x7 -> x12, waiting for transfers between devices: 0.11 us -> 75.1 us
    reduce_scatter x1 -> x3, waiting for transfers between devices: 118 us -> 192 us  [reduce_grads(): lax.psum_scatter(packed.reshape(tensor_size, GROUP, rows // GROUP, cols),...]
    reduce_scatter x1 -> x0, waiting for transfers between devices: 73.2 us -> none  [on_device(): lax.psum_scatter(total.astype(BF), 'tensor', scatter_dimension=0, tiled=T...]
    dot_general x33 -> x32, matrix products: 101 us -> 50.2 us  [product(): return lax.dot_general(left, right, dims, preferred_element_type=F32)]
    ppermute x0 -> x1, waiting for transfers between devices: none -> 46.9 us  [on_device(): other = lax.ppermute(other, 'tensor', [(i, i ^ 1) for i in range(T)])]
  transfers between devices with their start and end apart: 9 -> 12, of which waited for: 7 -> 10; matrix products, arithmetic and copies ran while one was open for 5% -> 7% of each run, Pallas kernels for 8% -> 0%
where the time goes in v2:
time: 826 us; the launch traced here: 816 us
  waiting for transfers between devices  429 us (52%)
  Pallas kernels  181 us (22%)
  blocking collectives  50.8 us (6%)
  matrix products  50.2 us (6%)
  local copies, waits for them, and re-layouts  49.7 us (6%)
  other arithmetic  39.9 us (5%)
  between operations  15 us (2%)
    reduce_scatter x3, waiting for transfers between devices, reduce_grads(): lax.psum_scatter(packed.reshape(tensor_size, GROUP, rows // GROUP, cols),...  192 us
    pallas_call x1, Pallas kernels, run_forward(): pl.pallas_call(forward_kernel, in_specs=[smem, anyw, vmem, vmem, vmem] +...  156 us
    reduce_scatter x4, waiting for transfers between devices, reduce_grads(): part = lax.psum_scatter(part, 'tensor', scatter_dimension=0, tiled=False)  82.6 us
    unnamed x12, waiting for transfers between devices  75.1 us
    dot_general x32, matrix products, product(): return lax.dot_general(left, right, dims, preferred_element_type=F32)  50.2 us
    ppermute x1, waiting for transfers between devices, on_device(): other = lax.ppermute(other, 'tensor', [(i, i ^ 1) for i in range(T)])  46.9 us
    psum x1, blocking collectives, on_device(): lax.psum(jnp.concatenate([sums[:3], sums2, jnp.stack(up_bias_parts), bias...  39.3 us
    all_gather x3, waiting for transfers between devices, reduce_grads(): lax.all_gather(part, 'dp', axis=0, tiled=True, axis_index_groups=dp_group...  31.5 us
  transfers between devices with their start and end apart: 12, of which 10 were waited for; matrix products, arithmetic and copies ran while one was open for 7% of the time, Pallas kernels for 0%

profile of v2, /device:TPU:0, one launch (start us, length us, event | category | flops | bytes accessed | tf_op | source)
XLA Modules:
  0.0 816.4 jit_solution(14058354837824573461)
XLA Ops:
  10.8 155.8 %forward.1 = (bf16[4,4,2,128,768]{4,3,2,1,0:T(8,128)(2,1)}, bf16[4,4,2,32,1024]{4,3,2,1,0:T(8,128)(2,1)}, bf16[4,4,2,128,1024]{4,3,2,1,0:T(8,128)(2,1)}, bf16[4,...) custom-call(s32[2]{0:T(128)} %len_ref.3, ...), custom_call_target="tpu_custom_call" | custom-call | flops 40000000000 | bytes 62914560 | tf_op jit(solution)/shard_map/forward/pallas_call | solution.py:579
  168.4 7.2 fusion.44
  198.2 25.3 %attend_back.1 = (bf16[4,512,256]{2,1,0:T(8,128)(2,1)}, f32[4,1024,256]{2,1,0:T(8,128)}, f32[4,1024,256]{2,1,0:T(8,128)}) custom-call(s32[2]{0:T(128)} %len_ref.3, bf16[4,512,256]{2,1,0:T(8,128)(2,1)} %get-tuple-element.44.q_ref, bf16[4,1024,256]{2,1,0:T(8,128)(2,1)} %get-tuple-element.45.k_ref, bf16[4,1024,256]{2,1,0:T(8,128)(2,1)} %get-tuple-element.46.v_ref, ...), custom_call_target="tpu_custom_call" | custom-call | tf_op jit(solution)/shard_map/attend_back/pallas_call | solution.py:646
  223.5 3.9 fusion.7
  228.0 46.9 %collective-permute-done = bf16[2,4,512,256]{3,2,1,0:T(8,128)(2,1)} collective-permute-done((bf16[2,4,512,256]{3,2,1,0:T(8,128)(2,1)}, bf16[2,4,512,256]{3,2,1,0:T(8,128)(2,1)}, u32[]{:S(2)}, u32[]{:S(2)}) %collective-permute-start) | collective-permute-done | bytes 2097184 | tf_op jit(solution)/shard_map/ppermute | solution.py:774
  291.5 3.9 stack.157
  295.4 4.1 stack.158
  299.5 3.9 stack.159
  303.4 3.9 stack.160
  307.3 6.5 pad_maximum_fusion.2
  343.0 75.0 %all-reduce.4.cloned.1.call-done = bf16[4,8,96,1024]{3,2,1,0:T(8,128)(2,1)} async-done(((bf16[4,8,96,1024]{3,2,1,0:T(8,128)(2,1)}), bf16[4,8,96,1024]{3,2,1,0:T(8,128)(2,1)}) %all-reduce.4.cloned.1.call-update) | async-done | bytes 6291472
  420.8 72.5 %reduce-scatter.17.cloned.1.call-done = bf16[4,1,128,1024]{3,2,0,1:T(8,128)(2,1)} async-done(((bf16[4,8,128,1024]{3,2,0,1:T(8,128)(2,1)}), bf16[4,1,128,1024]{3,2,0,1:T(8,128)(2,1)}) %reduce-scatter.17.cloned.1.call-update) | async-done | bytes 1048592 | tf_op jit(solution)/shard_map/reduce_scatter | solution.py:668
  493.3 74.7 %reduce-scatter.21.cloned.1.call-done = bf16[4,1,128,1024]{3,2,0,1:T(8,128)(2,1)} async-done(((bf16[4,8,128,1024]{3,2,0,1:T(8,128)(2,1)}), bf16[4,1,128,1024]{3,2,0,1:T(8,128)(2,1)}) %reduce-scatter.21.cloned.1.call-update) | async-done | bytes 1048592 | tf_op jit(solution)/shard_map/reduce_scatter | solution.py:668
  568.1 45.2 %reduce-scatter.13.cloned.1.call-done = bf16[4,1,32,1024]{3,2,0,1:T(8,128)(2,1)} async-done(((bf16[4,8,32,1024]{3,2,0,1:T(8,128)(2,1)}), bf16[4,1,32,1024]{3,2,0,1:T(8,128)(2,1)}) %reduce-scatter.13.cloned.1.call-update) | async-done | bytes 262160 | tf_op jit(solution)/shard_map/reduce_scatter | solution.py:668
  613.4 26.0 %reduce-scatter.11.cloned.1.call-done = bf16[1,96,1024]{2,1,0:T(8,128)(2,1)} async-done(((bf16[4,96,1024]{2,1,0:T(8,128)(2,1)}), bf16[1,96,1024]{2,1,0:T(8,128)(2,1)}) %reduce-scatter.11.cloned.1.call-update) | async-done | bytes 196624 | tf_op jit(solution)/shard_map/reduce_scatter | solution.py:675
  639.5 28.5 %reduce-scatter.19.cloned.1.call-done = bf16[1,128,1024]{2,1,0:T(8,128)(2,1)} async-done(((bf16[4,128,1024]{2,1,0:T(8,128)(2,1)}), bf16[1,128,1024]{2,1,0:T(8,128)(2,1)}) %reduce-scatter.19.cloned.1.call-update) | async-done | bytes 262160 | tf_op jit(solution)/shard_map/reduce_scatter | solution.py:675
  668.1 28.1 %reduce-scatter.23.cloned.1.call-done = bf16[1,128,1024]{2,1,0:T(8,128)(2,1)} async-done(((bf16[4,128,1024]{2,1,0:T(8,128)(2,1)}), bf16[1,128,1024]{2,1,0:T(8,128)(2,1)}) %reduce-scatter.23.cloned.1.call-update) | async-done | bytes 262160 | tf_op jit(solution)/shard_map/reduce_scatter | solution.py:675
  696.2 5.7 fusion.46
  702.0 39.3 %psum.7 = f32[14,1024]{1,0:T(8,128)S(1)} all-reduce(f32[14,1024]{1,0:T(8,128)S(1)} %concatenate.20), channel_id=1, replica_groups=mesh['dp'=8,'tensor'=4] {'dp','tensor'}, use_global_device_ids=true, to_apply=%region_12.13 | all-reduce | flops 14336 | bytes 114688 | tf_op jit(solution)/shard_map/psum | solution.py:796
  751.5 11.6 %all-gather.1 = bf16[1,256,1024]{2,1,0:T(8,128)(2,1)S(1)} all-gather(bf16[1,32,1024]{2,1,0:T(8,128)(2,1)} %reduce-scatter.15.cloned.1.call-done), channel_id=3, replica_groups={{0,4,8,12,16,20,24,28},{1,5,9,13,17,21,25,29},{2,6,10,14,18,22,26,30},{..., dimensions={1}, use_global_device_ids=true | all-gather | bytes 589824 | tf_op jit(solution)/shard_map/all_gather | solution.py:676
  768.7 5.6 all-gather.10.cloned.1.call-done
  774.4 4.1 bitcast_convert_fusion.1
  778.5 25.9 %all-gather.12.cloned.1.call-done = bf16[1,1024,1024]{2,1,0:T(8,128)(2,1)} async-done(((bf16[1,128,1024]{2,1,0:T(8,128)(2,1)}), bf16[1,1024,1024]{2,1,0:T(8,128)(2,1)}) %all-gather.12.cloned.1.call-update) | async-done | bytes 2097168 | tf_op jit(solution)/shard_map/all_gather | solution.py:676
  804.4 4.1 bitcast_convert_fusion
  (147 shorter events, 94.0 us)
Async XLA Ops:
  7.2 410.8 %all-reduce.4.cloned.1.call-start = ((), (), s32[]{:S(2)}) async-start(), calls=%async_computation.17 | async-start | bytes 12582912
  168.4 12.5 %copy-start.9 = (bf16[512,1024]{1,0:T(8,128)(2,1)}, bf16[512,1024]{1,0:T(8,128)(2,1)S(1)}, u32[]{:S(2)}) copy-start(bf16[512,1024]{1,0:T(8,128)(2,1)S(1)} %convert_element_type.139) | copy-start | bytes 3145732
  178.2 4.0 copy-start.22
  179.6 4.0 copy-start.23
  180.9 4.0 copy-start.25
  182.2 4.0 copy-start.11
  227.4 47.4 %collective-permute-start = (bf16[2,4,512,256]{3,2,1,0:T(8,128)(2,1)}, bf16[2,4,512,256]{3,2,1,0:T(8,128)(2,1)}, u32[]{:S(2)}, u32[]{:S(2)}) collective-permute-start(bf16[2,4,512,256]{3,2,1,0:T(8,128)(2,1)} %fusion.7), channel_id=1, source_target_pairs={{0,1},{1,0},{2,3},{3,2},{4,5},{5,4},{6,7},{7,6},{8,9},{9,8},{10,11... | collective-permute-start | bytes 6291464 | tf_op jit(solution)/shard_map/ppermute | solution.py:774
  279.4 3.3 copy-start.18
  280.1 9.2 %copy-start.3 = (bf16[4,512,768]{2,1,0:T(8,128)(2,1)}, bf16[4,512,768]{2,1,0:T(8,128)(2,1)S(1)}, u32[]{:S(2)}) copy-start(bf16[4,512,768]{2,1,0:T(8,128)(2,1)S(1)} %get-tuple-element.62) | copy-start | bytes 9437188
  313.8 179.4 %reduce-scatter.17.cloned.1.call-start = ((), (), s32[]{:S(2)}) async-start(), calls=%async_computation.10 | async-start | bytes 9437184 | tf_op jit(solution)/shard_map/reduce_scatter | solution.py:668
  324.9 243.1 %reduce-scatter.21.cloned.1.call-start = ((), (), s32[]{:S(2)}) async-start(), calls=%async_computation.12 | async-start | bytes 9437184 | tf_op jit(solution)/shard_map/reduce_scatter | solution.py:668
  325.2 3.0 copy-start.10
  325.2 3.3 copy-start.21
  336.3 277.0 %reduce-scatter.13.cloned.1.call-start = ((), (), s32[]{:S(2)}) async-start(), calls=%async_computation.8 | async-start | bytes 2359296 | tf_op jit(solution)/shard_map/reduce_scatter | solution.py:668
  341.8 297.6 %reduce-scatter.11.cloned.1.call-start = ((), (), s32[]{:S(2)}) async-start(), calls=%async_computation.7 | async-start | bytes 983040 | tf_op jit(solution)/shard_map/reduce_scatter | solution.py:675
  420.7 247.3 %copy-start.17 = (f32[8,1024]{1,0:T(8,128)S(1)}, f32[8,1024]{1,0:T(8,128)}, u32[]{:S(2)}) copy-start(f32[8,1024]{1,0:T(8,128)} %get-tuple-element.54) | copy-start | bytes 98308
  420.7 247.2 %reduce-scatter.19.cloned.1.call-start = ((), (), s32[]{:S(2)}) async-start(), calls=%async_computation.11 | async-start | bytes 1310720 | tf_op jit(solution)/shard_map/reduce_scatter | solution.py:675
  493.3 202.9 %reduce-scatter.23.cloned.1.call-start = ((), (), s32[]{:S(2)}) async-start(), calls=%async_computation.13 | async-start | bytes 1310720 | tf_op jit(solution)/shard_map/reduce_scatter | solution.py:675
  568.0 183.4 %reduce-scatter.15.cloned.1.call-start = ((), (), s32[]{:S(2)}) async-start(), calls=%async_computation.9 | async-start | bytes 327680 | tf_op jit(solution)/shard_map/reduce_scatter | solution.py:675
  613.4 150.8 %all-gather.8.cloned.1.call-start = ((), (), s32[]{:S(2)}) async-start(), calls=%async_computation.14 | async-start | bytes 1769472 | tf_op jit(solution)/shard_map/all_gather | solution.py:676
  639.4 135.0 %all-gather.10.cloned.1.call-start = ((), (), s32[]{:S(2)}) async-start(), calls=%async_computation.15 | async-start | bytes 2359296 | tf_op jit(solution)/shard_map/all_gather | solution.py:676
  668.0 136.3 %all-gather.12.cloned.1.call-start = ((), (), s32[]{:S(2)}) async-start(), calls=%async_computation.16 | async-start | bytes 2359296 | tf_op jit(solution)/shard_map/all_gather | solution.py:676
  743.2 3.1 copy-start.8
  778.4 30.0 %copy-start.13 = (bf16[512,1024]{1,0:T(8,128)(2,1)S(1)}, bf16[512,1024]{1,0:T(8,128)(2,1)}, u32[]{:S(2)}) copy-start(bf16[512,1024]{1,0:T(8,128)(2,1)} %get-tuple-element.126) | copy-start | bytes 3145732
  (16 other events, 31.8 us)
Sparse Core Ops, SparseCore 0:
  313.9 104.0 all-reduce.3
  421.9 71.3 reduce-scatter.16
  496.7 71.2 reduce-scatter.20
  572.1 41.2 reduce-scatter.12
  616.1 23.2 reduce-scatter.10
  641.5 26.4 reduce-scatter.18
  670.4 25.7 reduce-scatter.22
  698.5 18.2 reduce-scatter.14
  718.8 24.5 all-gather.7
  745.3 29.0 all-gather.9
  776.4 27.8 all-gather.11
